TPU v7x, 128 devices: a whole 4x4x4 slice. The times are simulated.
128 devices in a mesh: section: 8 (over x, core), ep: 16 (over y, z).
Axes of the slice: x: 4, y: 4, z: 4, core: 2. Of those that a mesh axis runs over, the one named last changes fastest.
Arguments:
- upstream: bfloat16 [8, 2048, 7168], P('section', 'ep'), may hold values from -6 to 6
- routes: int32 [8, 2048, 2], P('section', 'ep'), may hold values from 0 to 3, all different within a row; in each aligned block of 128 rows (0 to 127, 128 to 255, ..., all dimensions but the last counted through in order) at most 80 rows name the same one
- combine_weights: bfloat16 [8, 2048, 2], P('section', 'ep'), may hold values from 0.049804688 to 1
- gate_saved: bfloat16 [8, 16, 80, 4096], P('section', None, None, 'ep'), may hold values from -3 to 3
- up_saved: bfloat16 [8, 16, 80, 4096], P('section', None, None, 'ep'), may hold values from -3 to 3
- w_gate: bfloat16 [8, 7168, 4096], P('section', None, 'ep'), may hold values from -0.0625 to 0.0625
- w_up: bfloat16 [8, 7168, 4096], P('section', None, 'ep'), may hold values from -0.0625 to 0.0625
- w_down: bfloat16 [8, 4096, 7168], P('section', 'ep'), may hold values from -0.1875 to 0.1875
Outputs:
- grad_input: bfloat16 [8, 2048, 7168], P('section', 'ep')
- router_grad: float32 [8, 2048, 2], P('section', 'ep')
Inputs may be any that keep to these rules, and one draw needn't show every extreme that they name: `routes`: within the 128 tokens of one device (aligned blocks), no expert is named by more than 80 route entries, a bound that some block reaches; a token names 2 different experts.
All inputs are finite; a program needn't handle non-finite values.
Results may differ from a plain program's by a relative error of at most 0.005.
Values may be sent and summed in bfloat16 or wider, within the bound.
A program may use at most 192 MiB of HBM per device.

v0:
```python
import jax
import jax.numpy as jnp
from jax import lax
from jax.sharding import PartitionSpec as P

E_WIN = 4
TOPK = 2
CAP = 80


def from_behind(value, axis, by):
    devices = lax.axis_size(axis)
    return lax.ppermute(value, axis, [(i, (i + by) % devices) for i in range(devices)])


def slot_tables(routes_local, weights_local, tok_count):
    flat_routes = routes_local.reshape(-1)
    flat_weights = weights_local.reshape(-1)
    entries = flat_routes.shape[0]
    onehot = (flat_routes[:, None] == jnp.arange(E_WIN, dtype=jnp.int32)[None, :]).astype(jnp.int32)
    slot_rank = jnp.sum((jnp.cumsum(onehot, axis=0) - onehot) * onehot, axis=1)
    positions = flat_routes * CAP + slot_rank
    token_of = jnp.arange(entries, dtype=jnp.int32) // TOPK
    slot_token = jnp.full((E_WIN * CAP,), tok_count, jnp.int32).at[positions].set(token_of)
    slot_weight = jnp.zeros((E_WIN * CAP,), weights_local.dtype).at[positions].set(flat_weights)
    return (positions, slot_token, slot_weight)


def local(upstream, routes, combine_weights, gate_saved, up_saved, w_gate, w_up, w_down):
    incoming = from_behind(upstream, "section", -1)
    grad_local = incoming[0]
    tok_count = grad_local.shape[0]
    positions, slot_token, slot_weight = slot_tables(routes[0], combine_weights[0], tok_count)
    packed = jnp.take(grad_local, slot_token, axis=0, mode="fill", fill_value=0).reshape(
        E_WIN, CAP, -1
    )
    feature_width = packed.shape[-1]
    devices = lax.axis_size("ep")
    slices = devices // E_WIN
    weight_block = jnp.broadcast_to(
        slot_weight.reshape(E_WIN, 1, CAP), (E_WIN, slices, CAP)
    ).reshape(devices, CAP)
    spread_rows = jnp.broadcast_to(packed[:, None], (E_WIN, slices, CAP, feature_width)).reshape(
        devices, CAP, feature_width
    )
    arrived, arrived_weight = (
        lax.all_to_all(spread_rows, "ep", split_axis=0, concat_axis=0, tiled=True),
        lax.all_to_all(weight_block, "ep", split_axis=0, concat_axis=0, tiled=True),
    )
    gate_vals = gate_saved[0].astype(jnp.float32)
    up_vals = up_saved[0].astype(jnp.float32)
    back_grad = jnp.einsum("scd,hd->sch", arrived, w_down[0], preferred_element_type=jnp.float32)
    sigmoid_gate = jax.nn.sigmoid(gate_vals)
    silu_gate = gate_vals * sigmoid_gate
    hidden_act = silu_gate * up_vals
    router_part = jnp.sum(hidden_act * back_grad, axis=-1).astype(jnp.bfloat16)
    scaled = back_grad * arrived_weight.astype(jnp.float32)[:, :, None]
    grad_gate = (scaled * up_vals * sigmoid_gate * (1.0 + gate_vals * (1.0 - sigmoid_gate))).astype(
        jnp.bfloat16
    )
    grad_up = (scaled * silu_gate).astype(jnp.bfloat16)
    input_part = jnp.einsum("sch,dh->scd", grad_gate, w_gate[0], preferred_element_type=jnp.float32)
    input_part = (
        input_part + jnp.einsum("sch,dh->scd", grad_up, w_up[0], preferred_element_type=jnp.float32)
    ).astype(jnp.bfloat16)
    returned, router_back = (
        lax.all_to_all(input_part, "ep", split_axis=0, concat_axis=0, tiled=True),
        lax.all_to_all(router_part, "ep", split_axis=0, concat_axis=0, tiled=True),
    )
    summed = jnp.sum(
        returned.reshape(E_WIN, slices, CAP, feature_width).astype(jnp.float32), axis=1
    ).reshape(E_WIN * CAP, feature_width)
    router_sum = jnp.sum(
        router_back.reshape(E_WIN, slices, CAP).astype(jnp.float32), axis=1
    ).reshape(-1)
    combined = grad_local.astype(jnp.float32).at[slot_token].add(summed, mode="drop")
    grad_input = combined.astype(jnp.bfloat16)[None]
    router_grad = router_sum[positions].reshape(1, tok_count, TOPK)
    return (grad_input, router_grad)


def solution(mesh):
    in_specs = (
        P("section", "ep", None),
        P("section", "ep", None),
        P("section", "ep", None),
        P("section", None, None, "ep"),
        P("section", None, None, "ep"),
        P("section", None, "ep"),
        P("section", None, "ep"),
        P("section", "ep", None),
    )
    out_specs = (P("section", "ep", None), P("section", "ep", None))
    return jax.shard_map(local, mesh=mesh, in_specs=in_specs, out_specs=out_specs, check_vma=False)
```

profile of v0, /device:TPU:7, one launch (start us, length us, event | category | flops | bytes accessed | tf_op | source)
XLA Modules:
  0.0 828.9 jit_solution(14779038632802579331)
XLA Ops:
  0.6 0.7 collective-permute-start
  1.3 0.8 copy.27
  2.4 1.2 reduce-window.6
  4.9 0.8 copy.31
  5.9 2.2 scatter_custom_fusion.1
  8.8 7.8 all-to-all-start.1
  16.6 1.4 scatter_custom_fusion
  18.1 6.6 collective-permute-done
  24.7 6.1 gather_fusion
  30.8 4.8 broadcast_select_fusion
  35.6 8.0 broadcast_in_dim.42
  43.7 7.8 all-to-all-start
  51.5 334.0 %all-to-all-done = bf16[16,80,7168]{2,1,0:T(8,128)(2,1)} async-done(((bf16[16,80,7168]{2,1,0:T(8,128)(2,1)}), bf16[16,80,7168]{2,1,0:T(8,128)(2,1)}, u32[]{:S(2)}, u32[]{:S(2)}) %all-to-all-start) | async-done | bytes 18350112 | tf_op jit(solution)/shard_map/all_to_all | solution.py:47
  385.5 13.1 %fusion.9 = (bf16[16,80]{1,0:T(8,128)(2,1)S(1)}, f32[16,80,256]{2,1,0:T(8,128)S(1)}) fusion(bf16[1,16,80,256]{3,2,1,0:T(8,128)(2,1)} %param.12, bf16[1,16,80,256]{3,2,1,0:T(8,128)(2,1)} %param.11, bf16[16,80,7168]{2,1,0:T(8,128)(2,1)} %all-to-all-done, bf16[1,256,7168]{2,1,0:T(8,128)(2,1)} %param.15), kind=kOutput, calls=%fused_computation.23 | convolution fusion | flops 4700568576 | bytes 24644096 | tf_op jit(solution)/shard_map/scd,hd->sch/dot_general | solution.py:52
  399.2 7.0 all-to-all-start.3
  406.2 19.8 %fusion.1 = f32[16,80,7168]{2,1,0:T(8,128)} fusion(bf16[1,7168,256]{2,1,0:T(8,128)(2,1)} %param.13, f32[16,80,256]{2,1,0:T(8,128)S(1)} %get-tuple-element.9, bf16[1,16,80,256]{3,2,1,0:T(8,128)(2,1)} %param.12, bf16[1,16,80,256]{3,2,1,0:T(8,128)(2,1)} %param.11, f32[16,80]{1,0:T(8,128)S(1)} %bitcast.75), kind=kOutput, calls=%fused_computation.9 | convolution fusion | flops 4701880320 | bytes 42996736 | tf_op jit(solution)/shard_map/sch,dh->scd/dot_general | solution.py:62
  426.0 22.1 %add_convert_fusion = bf16[16,80,7168]{2,1,0:T(8,128)(2,1)} fusion(f32[16,80,7168]{2,1,0:T(8,128)} %fusion.1, bf16[1,7168,256]{2,1,0:T(8,128)(2,1)} %param.14, f32[16,80,256]{2,1,0:T(8,128)S(1)} %get-tuple-element.9, f32[16,80]{1,0:T(8,128)S(1)} %bitcast.76, bf16[1,16,80,256]{3,2,1,0:T(8,128)(2,1)} %param.11), kind=kOutput, calls=%fused_computation.6 | convolution fusion | flops 4718592000 | bytes 60691456 | tf_op jit(solution)/shard_map/sch,dh->scd/dot_general | solution.py:64
  448.1 6.7 all-to-all-start.2
  454.8 2.3 bitcast_convert_fusion
  457.2 1.9 gather_fusion.1
  459.9 333.6 %all-to-all-done.2 = bf16[16,80,7168]{2,1,0:T(8,128)(2,1)} async-done(((bf16[16,80,7168]{2,1,0:T(8,128)(2,1)}), bf16[16,80,7168]{2,1,0:T(8,128)(2,1)}, u32[]{:S(2)}, u32[]{:S(2)}) %all-to-all-start.2) | async-done | bytes 18350112 | tf_op jit(solution)/shard_map/all_to_all | solution.py:67
  793.5 13.6 %convert_reduce_fusion = f32[4,80,7168]{2,1,0:T(8,128)} fusion(bf16[16,80,7168]{2,1,0:T(8,128)(2,1)} %all-to-all-done.2), kind=kLoop, calls=%fused_computation.5 | loop fusion | flops 16056320 | bytes 27525120 | tf_op jit(solution)/shard_map/reduce_sum | solution.py:70
  807.1 18.4 %scatter_fusion = f32[128,7168]{1,0:T(8,128)} fusion(f32[128,7168]{1,0:T(8,128)} %bitcast_convert_fusion, s32[320]{0:T(512)S(1)} %compare_select_fusion.1, f32[320,7168]{1,0:T(8,128)} %bitcast.73), kind=kCustom, calls=%fused_computation.4 | custom fusion | flops 2293760 | bytes 27526400 | tf_op jit(solution)/shard_map/scatter-add | solution.py:76
  825.4 3.5 convert_bitcast_fusion
  (33 shorter events, 4.1 us)
Async XLA Ops:
  0.6 24.1 %collective-permute-start = (bf16[1,128,7168]{2,1,0:T(8,128)(2,1)}, bf16[1,128,7168]{2,1,0:T(8,128)(2,1)S(1)}, u32[]{:S(2)}, u32[]{:S(2)}) collective-permute-start(bf16[1,128,7168]{2,1,0:T(8,128)(2,1)} %param.8), channel_id=1, source_target_pairs={{0,112},{16,0},{32,16},{48,32},{64,48},{80,64},{96,80},{112,96},{1... | collective-permute-start | bytes 5505032 | tf_op jit(solution)/shard_map/ppermute | solution.py:13
  8.8 26.9 %all-to-all-start.1 = ((bf16[16,1,80]{2,1,0:T(2,128)(2,1)}), bf16[16,1,80]{2,1,0:T(2,128)(2,1)S(1)}, u32[]{:S(2)}, u32[]{:S(2)}) async-start(bf16[16,1,80]{2,1,0:T(2,128)(2,1)} %copy.32), calls=%async_computation.1 | async-start | bytes 16384 | tf_op jit(solution)/shard_map/all_to_all | solution.py:48
  43.7 341.8 %all-to-all-start = ((bf16[16,80,7168]{2,1,0:T(8,128)(2,1)}), bf16[16,80,7168]{2,1,0:T(8,128)(2,1)}, u32[]{:S(2)}, u32[]{:S(2)}) async-start(bf16[16,80,7168]{2,1,0:T(8,128)(2,1)} %bitcast.72), calls=%async_computation | async-start | bytes 36700160 | tf_op jit(solution)/shard_map/all_to_all | solution.py:47
  399.2 48.9 %all-to-all-start.3 = ((bf16[16,1,80]{2,1,0:T(2,128)(2,1)}), bf16[16,1,80]{2,1,0:T(2,128)(2,1)S(1)}, u32[]{:S(2)}, u32[]{:S(2)}) async-start(bf16[16,1,80]{2,1,0:T(2,128)(2,1)} %copy.33), calls=%async_computation.3 | async-start | bytes 16384 | tf_op jit(solution)/shard_map/all_to_all | solution.py:68
  448.1 345.4 %all-to-all-start.2 = ((bf16[16,80,7168]{2,1,0:T(8,128)(2,1)}), bf16[16,80,7168]{2,1,0:T(8,128)(2,1)}, u32[]{:S(2)}, u32[]{:S(2)}) async-start(bf16[16,80,7168]{2,1,0:T(8,128)(2,1)} %add_convert_fusion), calls=%async_computation.2 | async-start | bytes 36700160 | tf_op jit(solution)/shard_map/all_to_all | solution.py:67
where the time goes:
time: 830 us; the launch traced here: 829 us
  waiting for transfers between devices  674 us (81%)
  matrix products  54.9 us (7%)
  other arithmetic  44.7 us (5%)
  starting transfers between devices  30 us (4%)
  local copies, waits for them, and re-layouts  24.4 us (3%)
    all_to_all x1, waiting for transfers between devices, local(): lax.all_to_all(spread_rows, 'ep', split_axis=0, concat_axis=0, tiled=True)  334 us
    all_to_all x1, waiting for transfers between devices, local(): lax.all_to_all(input_part, 'ep', split_axis=0, concat_axis=0, tiled=True)  334 us
    dot_general x1, matrix products, local(): jnp.einsum('sch,dh->scd', grad_up, w_up[0], preferred_element_type=jnp.fl...  22.1 us
    dot_general x1, matrix products, local(): jnp.einsum('sch,dh->scd', grad_gate, w_gate[0], preferred_element_type=jn...  19.8 us
    scatter-add x1, other arithmetic, local(): grad_local.astype(jnp.float32).at[slot_token].add(summed, mode='drop')  18.4 us
  transfers between devices with their start and end apart: 5, of which 3 were waited for; matrix products, arithmetic and copies ran while one was open for 8% of the time, Pallas kernels for 0%

commit v1 on v0

v1 whole, which is shorter than its diff:
```python
import functools

import jax
import jax.numpy as jnp
from jax import lax
from jax.experimental import pallas as pl
from jax.experimental.pallas import tpu as pltpu
from jax.sharding import PartitionSpec as P

MESH = pl.DeviceIdType.MESH
BF = jnp.bfloat16
F32 = jnp.float32

SECTIONS = 8
E_WIN = 4
SLICES = 4
TOPK = 2
CAP = 80
TOK = 128
D = 7168
HID = 256
Q = D // SLICES
ROWS = SLICES * CAP

CW = 512
CA = 4096
NA = CA // CW
HA = NA // 2
NB = (D - CA) // CW
HB = NB // 2
RT = 128
WA = CA + RT
BCOL = WA
WB = D - CA


def dot_nt(a, b):
    return lax.dot_general(a, b, (((1,), (1,)), ((), ())), preferred_element_type=F32)


def place():
    s = lax.axis_index("section")
    p = lax.axis_index("ep")
    return s, p // SLICES, lax.rem(p, SLICES)


def shifted(a, by, n):
    return lax.rem(a + by + n, n)


def cols(start, width):
    return pl.ds(pl.multiple_of(start, 128), width)


def remote(src, dst, send, recv, device):
    return pltpu.make_async_remote_copy(
        src_ref=src, dst_ref=dst, send_sem=send, recv_sem=recv, device_id=device, device_id_type=MESH
    )


def dispatch_kernel(
    up, wd, pick, cot, bp,
    tok, slots, recv, wdr, ps,
    tok_s, tok_r, wd_s, wd_r, cot_s, cot_r, y_s, y_r, b_s, b_r, loc,
):
    s, y, z = place()
    behind = shifted(s, -1, SECTIONS)
    ahead = shifted(s, 1, SECTIONS)

    def dev(section, yy, zz):
        return (section, yy * SLICES + zz)

    barrier = pltpu.get_barrier_semaphore()
    for k in range(SLICES):
        pl.semaphore_signal(barrier, inc=1, device_id=dev(ahead, y, k), device_id_type=MESH)
    for k in range(1, SLICES):
        pl.semaphore_signal(barrier, inc=1, device_id=dev(s, y, shifted(z, k, SLICES)), device_id_type=MESH)
        pl.semaphore_signal(barrier, inc=1, device_id=dev(s, shifted(y, k, E_WIN), z), device_id_type=MESH)
    pl.semaphore_wait(barrier, 10)

    def tok_copy(k, owner):
        q = shifted(z, k, SLICES)
        return remote(up.at[:, cols(q * Q, Q)], tok.at[owner], tok_s.at[k], tok_r.at[k], dev(behind, y, q))

    def wd_copy(k, owner):
        q = shifted(z, k, SLICES)
        return remote(wd.at[:, cols(q * Q, Q)], wdr.at[owner], wd_s.at[k], wd_r.at[k], dev(s, y, q))

    cot_copy = remote(up, cot, cot_s, cot_r, dev(behind, y, z))
    wd_own = pltpu.make_async_copy(wd.at[:, cols(z * Q, Q)], wdr.at[z], loc.at[0])

    def y_copy(k, m, source, owner):
        return remote(
            slots.at[k, m], recv.at[owner, source], y_s.at[k, m], y_r.at[k, m], dev(s, shifted(y, k, E_WIN), z)
        )

    def b_copy(k, m, yb, owner):
        return remote(
            ps.at[k, yb], bp.at[owner, yb], b_s.at[k, m], b_r.at[k, m], dev(s, y, shifted(z, k, SLICES))
        )

    for k in (2, 1, 3, 0):
        tok_copy(k, z).start()
    wd_own.start()

    order = (0, 1, 3, 2)
    for m in order:
        source = shifted(z, -m, SLICES)
        tok_copy(m, source).wait_recv()

        def pack(k, _):
            e = shifted(y, k, E_WIN)
            rows = jnp.dot(pick[source, e], tok[source], preferred_element_type=F32).astype(BF)
            slots[k, m] = rows
            y_copy(k, m, source, y).start()
            return 0

        lax.fori_loop(1, E_WIN, pack, 0)
        recv[y, source] = jnp.dot(pick[source, y], tok[source], preferred_element_type=F32).astype(BF)
        if m == order[-1]:
            for k in (2, 1, 3):
                wd_copy(k, z).start()
            cot_copy.start()

    wd_own.wait()
    for k in (1, 3, 2):
        wd_copy(k, shifted(z, -k, SLICES)).wait_recv()

    own = []
    for m in (0, 1, 3, 2):
        yb = shifted(y, -m, E_WIN)
        if m:
            for j in order:
                y_copy(m, j, shifted(z, -j, SLICES), yb).wait_recv()

        def partial_grad(k, _):
            h = shifted(z, k, SLICES)
            part = dot_nt(recv[yb].reshape(ROWS, Q), wdr[h])
            ps[k, yb] = part.astype(BF).reshape(SLICES, CAP, HID)
            b_copy(k, m, yb, z).start()
            return 0

        lax.fori_loop(1, SLICES, partial_grad, 0)
        part = dot_nt(recv[yb].reshape(ROWS, Q), wdr[z])
        ps[0, yb] = part.astype(BF).reshape(SLICES, CAP, HID)
        copy = pltpu.make_async_copy(ps.at[0, yb], bp.at[z, yb], loc.at[1 + m])
        copy.start()
        own.append(copy)

    for copy in own:
        copy.wait()
    for k in range(SLICES):
        tok_copy(k, z).wait_send()
    cot_copy.wait()
    for k in range(1, SLICES):
        wd_copy(k, z).wait_send()
        for m in range(SLICES):
            y_copy(k, m, shifted(z, -m, SLICES), y).wait_send()
        for m in range(E_WIN):
            yb = shifted(y, -m, E_WIN)
            b_copy(k, m, yb, z).wait_send()
            b_copy(k, m, yb, shifted(z, -k, SLICES)).wait_recv()


def return_kernel(
    bp, gate, upv, sw, wg, wu, cot, spread, spread_k, out, router,
    grads, weights, partial, r1p, r1m, r2p, r2m, arecv, brecv, ctok, rb1p, rb1m, rb2p, rb2m,
    w_sem, r1_s, r1_r, r2p_s, r2p_r, r2m_s, r2m_r, ay_s, ay_r, by_s, by_r, b1_s, b1_r, b2p_s, b2p_r, b2m_s, b2m_r,
):
    s, y, z = place()
    zp, zm, z2 = shifted(z, 1, SLICES), shifted(z, -1, SLICES), shifted(z, 2, SLICES)
    right, left = (s, y * SLICES + zp), (s, y * SLICES + zm)

    def along_y(k):
        return (s, shifted(y, k, E_WIN) * SLICES + z)

    def w_copy(c):
        take = pl.ds(c * CW, CW)
        return (
            pltpu.make_async_copy(wg.at[take], weights.at[c, :, pl.ds(0, HID)], w_sem.at[0, c]),
            pltpu.make_async_copy(wu.at[take], weights.at[c, :, pl.ds(HID, HID)], w_sem.at[1, c]),
        )

    def start_weights(c, _):
        for copy in w_copy(c):
            copy.start()
        return 0

    lax.fori_loop(0, D // CW, start_weights, 0)

    barrier = pltpu.get_barrier_semaphore()
    for device in (right, left, along_y(1), along_y(2), along_y(3)):
        pl.semaphore_signal(barrier, inc=1, device_id=device, device_id_type=MESH)

    def elementwise(b, _):
        back = bp[0, b].astype(F32)
        for k in range(1, SLICES):
            back = back + bp[k, b].astype(F32)
        g = gate[b].astype(F32)
        u = upv[b].astype(F32)
        sig = 1.0 / (1.0 + jnp.exp(-g))
        silu = g * sig
        part = jnp.sum(silu * u * back, axis=-1, keepdims=True)
        lane = lax.broadcasted_iota(jnp.int32, (SLICES, CAP, RT), 2)
        partial[b, :, :, pl.ds(CA, RT)] = jnp.where(lane == z, part, 0.0).astype(BF)
        scaled = back * sw[b]
        grad_gate = (scaled * u * sig * (1.0 + g * (1.0 - sig))).astype(BF)
        grad_up = (scaled * silu).astype(BF)
        grads[b, :, pl.ds(0, HID)] = grad_gate.reshape(ROWS, HID)
        grads[b, :, pl.ds(HID, HID)] = grad_up.reshape(ROWS, HID)
        return 0

    lax.fori_loop(0, E_WIN, elementwise, 0)

    pl.semaphore_wait(barrier, 5)

    def first(half, col, width, i):
        src = partial.at[:, z2, :, cols(col, width)]
        if half == 0:
            return remote(src, r1p.at[:, :, cols(col, width)], r1_s.at[i], r1_r.at[i], right)
        return remote(src, r1m.at[:, :, cols(col - CA // 2, width)], r1_s.at[i], r1_r.at[i], left)

    def to_right(col, width, i):
        src = partial.at[:, zp, :, cols(col, width)]
        return remote(src, r2p.at[:, :, cols(col, width)], r2p_s.at[i], r2p_r.at[i], right)

    def to_left(col, width, i):
        src = partial.at[:, zm, :, cols(col, width)]
        return remote(src, r2m.at[:, :, cols(col, width)], r2m_s.at[i], r2m_r.at[i], left)

    def a_copy(k, col, width, i):
        src = partial.at[shifted(y, k, E_WIN), z, :, cols(col, width)]
        return remote(src, arecv.at[y, :, cols(col, width)], ay_s.at[k, i], ay_r.at[k, i], along_y(k))

    def b_copy(k, j):
        src = partial.at[shifted(y, k, E_WIN), :, :, cols(BCOL + j * CW, CW)]
        return remote(src, brecv.at[:, y, :, cols(j * CW, CW)], by_s.at[k, j], by_r.at[k, j], along_y(k))

    def b_first(half, j):
        src = ctok.at[z2, :, cols(j * CW, CW)]
        if half == 0:
            return remote(src, rb1p.at[:, cols(j * CW, CW)], b1_s.at[j], b1_r.at[j], right)
        return remote(src, rb1m.at[:, cols((j - HB) * CW, CW)], b1_s.at[j], b1_r.at[j], left)

    def b_right(j):
        return remote(ctok.at[zp, :, cols(j * CW, CW)], rb2p.at[:, cols(j * CW, CW)], b2p_s.at[j], b2p_r.at[j], right)

    def b_left(j):
        return remote(ctok.at[zm, :, cols(j * CW, CW)], rb2m.at[:, cols(j * CW, CW)], b2m_s.at[j], b2m_r.at[j], left)

    first(1, CA, RT, NA).start()
    to_right(CA, RT, NA).start()

    def input_part(c, col):
        for copy in w_copy(c):
            copy.wait()

        def block(b, _):
            part = dot_nt(grads[b], weights[c])
            partial[b, :, :, cols(col, CW)] = part.astype(BF).reshape(SLICES, CAP, CW)
            return 0

        lax.fori_loop(0, E_WIN, block, 0)

    def produce_a(c, half):
        input_part(c, c * CW)
        first(half, c * CW, CW, c).start()
        if half == 0:
            to_left(c * CW, CW, c).start()
        else:
            to_right(c * CW, CW, c).start()

    def produce_b(j):
        input_part(NA + j, BCOL + j * CW)
        for k in (2, 1, 3):
            b_copy(k, j).start()
        brecv[:, y, :, cols(j * CW, CW)] = partial[y, :, :, cols(BCOL + j * CW, CW)]

    def produce(i, _):
        produce_a(i, 0)
        produce_a(HA + i, 1)
        produce_b(i)
        return 0

    lax.fori_loop(0, HA, produce, 0)

    def produce_rest(j, _):
        produce_b(j)
        return 0

    lax.fori_loop(HA, NB, produce_rest, 0)

    def relay(half, col, width, i):
        first(half, col, width, i).wait_recv()
        if half == 0:
            mine, other = partial.at[:, zp, :, cols(col, width)], r1p.at[:, :, cols(col, width)]
        else:
            mine, other = partial.at[:, zm, :, cols(col, width)], r1m.at[:, :, cols(col - CA // 2, width)]
        mine[...] = (mine[...].astype(F32) + other[...].astype(F32)).astype(BF)
        if half == 0:
            to_right(col, width, i).start()
        else:
            to_left(col, width, i).start()

    relay(1, CA, RT, NA)

    def relay_pair(i, _):
        relay(0, i * CW, CW, i)
        relay(1, (HA + i) * CW, CW, HA + i)
        return 0

    lax.fori_loop(0, HA, relay_pair, 0)

    def finish_a(col, width, i):
        to_right(col, width, i).wait_recv()
        to_left(col, width, i).wait_recv()
        mine = partial.at[:, z, :, cols(col, width)]
        total = mine[...].astype(F32) + r2p[:, :, cols(col, width)].astype(F32) + r2m[:, :, cols(col, width)].astype(F32)
        mine[...] = total.astype(BF)
        for k in (2, 1, 3):
            a_copy(k, col, width, i).start()
        arecv[y, :, cols(col, width)] = partial[y, z, :, cols(col, width)]

    def tokens_b(half, j):
        for k in (1, 3, 2):
            b_copy(k, j).wait_recv()

        def combine(zz, _):
            rows = brecv[zz, :, :, cols(j * CW, CW)].reshape(E_WIN * CAP, CW)
            ctok[zz, :, cols(j * CW, CW)] = jnp.dot(spread[zz], rows, preferred_element_type=F32).astype(BF)
            return 0

        lax.fori_loop(0, SLICES, combine, 0)
        b_first(half, j).start()
        if half == 0:
            b_left(j).start()
        else:
            b_right(j).start()

    finish_a(CA, RT, NA)

    def second(i, _):
        tokens_b(0, i)
        finish_a(i * CW, CW, i)
        tokens_b(1, HB + i)
        finish_a((HA + i) * CW, CW, HA + i)
        return 0

    lax.fori_loop(0, HB, second, 0)
    for i in range(HB, HA):
        finish_a(i * CW, CW, i)
        finish_a((HA + i) * CW, CW, HA + i)

    def relay_b(half, j):
        b_first(half, j).wait_recv()
        if half == 0:
            mine, other = ctok.at[zp, :, cols(j * CW, CW)], rb1p.at[:, cols(j * CW, CW)]
        else:
            mine, other = ctok.at[zm, :, cols(j * CW, CW)], rb1m.at[:, cols((j - HB) * CW, CW)]
        mine[...] = (mine[...].astype(F32) + other[...].astype(F32)).astype(BF)
        if half == 0:
            b_right(j).start()
        else:
            b_left(j).start()

    def relay_b_pair(i, _):
        relay_b(0, i)
        relay_b(1, HB + i)
        return 0

    lax.fori_loop(0, HB, relay_b_pair, 0)

    for k in range(1, E_WIN):
        a_copy(k, CA, RT, NA).wait_recv()
    parts = arecv[:, :, pl.ds(CA, RT)].reshape(E_WIN * CAP, RT)
    for k in range(TOPK):
        values = jnp.dot(spread_k[k], parts, preferred_element_type=F32)
        router[:, pl.ds(k, 1)] = jnp.sum(values, axis=-1, keepdims=True)

    def last_a(c, _):
        for k in (1, 3, 2):
            a_copy(k, c * CW, CW, c).wait_recv()
        rows = arecv[:, :, cols(c * CW, CW)].reshape(E_WIN * CAP, CW)
        total = jnp.dot(spread[z], rows, preferred_element_type=F32)
        out[:, cols(c * CW, CW)] = (cot[:, cols(c * CW, CW)].astype(F32) + total).astype(BF)
        return 0

    lax.fori_loop(0, NA, last_a, 0)

    def last_b(j, _):
        b_right(j).wait_recv()
        b_left(j).wait_recv()
        take = cols(j * CW, CW)
        total = ctok[z, :, take].astype(F32) + rb2p[:, take].astype(F32) + rb2m[:, take].astype(F32)
        out[:, cols(CA + j * CW, CW)] = (cot[:, cols(CA + j * CW, CW)].astype(F32) + total).astype(BF)
        return 0

    lax.fori_loop(0, NB, last_b, 0)

    def sent_a(half, col, width, i):
        first(half, col, width, i).wait_send()
        to_right(col, width, i).wait_send()
        to_left(col, width, i).wait_send()
        for k in range(1, E_WIN):
            a_copy(k, col, width, i).wait_send()

    def sent_a_pair(i, _):
        sent_a(0, i * CW, CW, i)
        sent_a(1, (HA + i) * CW, CW, HA + i)
        return 0

    lax.fori_loop(0, HA, sent_a_pair, 0)
    sent_a(1, CA, RT, NA)

    def sent_b(half, j):
        for k in range(1, E_WIN):
            b_copy(k, j).wait_send()
        b_first(half, j).wait_send()
        b_right(j).wait_send()
        b_left(j).wait_send()

    def sent_b_pair(i, _):
        sent_b(0, i)
        sent_b(1, HB + i)
        return 0

    lax.fori_loop(0, HB, sent_b_pair, 0)


def vmem(*shape, dtype=BF):
    return pltpu.VMEM(shape, dtype)


def sems(*shape):
    return pltpu.SemaphoreType.DMA(shape)


ANY = pl.BlockSpec(memory_space=pl.ANY)
VM = pl.BlockSpec(memory_space=pltpu.VMEM)


def dispatch(upstream, w_down, pick):
    return pl.pallas_call(
        dispatch_kernel,
        out_shape=(
            jax.ShapeDtypeStruct((TOK, D), BF),
            jax.ShapeDtypeStruct((SLICES, E_WIN, SLICES, CAP, HID), BF),
        ),
        in_specs=[ANY, ANY, VM],
        out_specs=(ANY, ANY),
        scratch_shapes=[
            vmem(SLICES, TOK, Q),
            vmem(E_WIN, SLICES, CAP, Q),
            vmem(E_WIN, SLICES, CAP, Q),
            vmem(SLICES, HID, Q),
            vmem(SLICES, E_WIN, SLICES, CAP, HID),
            sems(SLICES), sems(SLICES),
            sems(SLICES), sems(SLICES),
            pltpu.SemaphoreType.DMA, pltpu.SemaphoreType.DMA,
            sems(E_WIN, SLICES), sems(E_WIN, SLICES),
            sems(SLICES, E_WIN), sems(SLICES, E_WIN),
            sems(1 + E_WIN),
        ],
        compiler_params=pltpu.CompilerParams(collective_id=0, has_side_effects=True, vmem_limit_bytes=40 * 2**20),
        name="dispatch",
    )(upstream, w_down, pick)


def give_back(bp, gate, up, sw, w_gate, w_up, cot, spread, spread_k):
    return pl.pallas_call(
        return_kernel,
        out_shape=(
            jax.ShapeDtypeStruct((TOK, D), BF),
            jax.ShapeDtypeStruct((TOK, TOPK), F32),
        ),
        in_specs=[VM, VM, VM, VM, ANY, ANY, VM, VM, VM],
        out_specs=(VM, VM),
        scratch_shapes=[
            vmem(E_WIN, ROWS, 2 * HID),
            vmem(D // CW, CW, 2 * HID),
            vmem(E_WIN, SLICES, CAP, D + RT),
            vmem(E_WIN, CAP, CA // 2),
            vmem(E_WIN, CAP, CA // 2 + RT),
            vmem(E_WIN, CAP, WA),
            vmem(E_WIN, CAP, WA),
            vmem(E_WIN, CAP, WA),
            vmem(SLICES, E_WIN, CAP, WB),
            vmem(SLICES, TOK, WB),
            vmem(TOK, WB // 2),
            vmem(TOK, WB // 2),
            vmem(TOK, WB),
            vmem(TOK, WB),
            sems(2, D // CW),
            sems(NA + 1), sems(NA + 1),
            sems(NA + 1), sems(NA + 1),
            sems(NA + 1), sems(NA + 1),
            sems(E_WIN, NA + 1), sems(E_WIN, NA + 1),
            sems(E_WIN, NB), sems(E_WIN, NB),
            sems(NB), sems(NB),
            sems(NB), sems(NB),
            sems(NB), sems(NB),
        ],
        compiler_params=pltpu.CompilerParams(collective_id=1, has_side_effects=True, vmem_limit_bytes=63 * 2**20),
        name="give_back",
    )(bp, gate, up, sw, w_gate, w_up, cot, spread, spread_k)


def local(upstream, routes, combine_weights, gate_saved, up_saved, w_gate, w_up, w_down):
    p = lax.axis_index("ep")
    y, z = p // SLICES, lax.rem(p, SLICES)
    info = jnp.concatenate([routes[0].astype(F32).T, combine_weights[0].astype(F32).T], axis=0)
    gathered = lax.all_gather(info, "ep")
    named = gathered[:, :TOPK]
    gains = gathered[:, TOPK:]
    experts = jnp.arange(E_WIN, dtype=F32)
    hit = (named[:, :, None, :] == experts[None, None, :, None]).sum(axis=1)
    before = jnp.triu(jnp.ones((TOK, TOK), BF), 1)
    rank = jnp.einsum("set,tu->seu", hit.astype(BF), before, preferred_element_type=F32)
    slot = jnp.where(hit > 0, rank, -1.0)
    slots = jnp.arange(CAP, dtype=F32)
    mine = lax.dynamic_index_in_dim(slot, y, 1, keepdims=False)
    gain = jnp.sum(jnp.where(named == y.astype(F32), gains, 0.0), axis=1)
    slot_weight = jnp.sum(jnp.where(mine[:, None, :] == slots[None, :, None], gain[:, None, :], 0.0), axis=-1)
    row = lax.dynamic_slice_in_dim(slot, y * SLICES, SLICES, 0)
    pick = (row[:, :, None, :] == slots[None, None, :, None]).astype(BF)
    spread = (jnp.swapaxes(row, 1, 2)[:, :, :, None] == slots[None, None, None, :]).astype(BF)
    own = lax.dynamic_index_in_dim(spread, z, 0, keepdims=False)
    chosen = routes[0].T[:, :, None, None] == jnp.arange(E_WIN, dtype=jnp.int32)[None, None, :, None]
    spread_k = jnp.where(chosen, own[None], 0).astype(BF).reshape(TOPK, TOK, E_WIN * CAP)

    cot, bp = dispatch(upstream[0], w_down[0], pick)
    grad_input, router_grad = give_back(
        bp,
        gate_saved[0].reshape(E_WIN, SLICES, CAP, HID),
        up_saved[0].reshape(E_WIN, SLICES, CAP, HID),
        slot_weight.reshape(E_WIN, SLICES, CAP, 1),
        w_gate[0],
        w_up[0],
        cot,
        spread.reshape(SLICES, TOK, E_WIN * CAP),
        spread_k,
    )
    return grad_input[None], router_grad[None]


def solution(mesh):
    in_specs = (
        P("section", "ep", None),
        P("section", "ep", None),
        P("section", "ep", None),
        P("section", None, None, "ep"),
        P("section", None, None, "ep"),
        P("section", None, "ep"),
        P("section", None, "ep"),
        P("section", "ep", None),
    )
    out_specs = (P("section", "ep", None), P("section", "ep", None))
    return jax.shard_map(local, mesh=mesh, in_specs=in_specs, out_specs=out_specs, check_vma=False)
```

time: 830 us -> 275 us (0.33)
  waiting for transfers between devices: 674 us -> 0 us
  Pallas kernels: 0 us -> 236 us
  matrix products: 54.9 us -> 0.13 us
  other arithmetic: 44.7 us -> 4.09 us
  starting transfers between devices: 30 us -> 0 us
  blocking collectives: 0 us -> 19.3 us
  local copies, waits for them, and re-layouts: 24.4 us -> 12.9 us
    all_to_all x4 -> x0, waiting for transfers between devices: 668 us -> none  [the longest x1 334 us: local(): lax.all_to_all(spread_rows, 'ep', split_axis=0, concat_axis=0, tiled=True)]
    pallas_call x0 -> x2, Pallas kernels: none -> 236 us  [the longest x1 129 us: give_back(): pl.pallas_call(return_kernel, out_shape=(jax.ShapeDtypeStruct((TOK, D), B...]
    dot_general x3 -> x1, matrix products: 54.9 us -> 0.13 us  [local(): jnp.einsum('set,tu->seu', hit.astype(BF), before, preferred_element_type=...]
    all_to_all x4 -> x0, starting transfers between devices: 29.3 us -> none  [the longest x1 7.81 us: local(): lax.all_to_all(spread_rows, 'ep', split_axis=0, concat_axis=0, tiled=True)]
    all_gather x0 -> x1, blocking collectives: none -> 19.3 us  [local(): gathered = lax.all_gather(info, 'ep')]
    scatter-add x1 -> x0, other arithmetic: 18.4 us -> none  [local(): grad_local.astype(jnp.float32).at[slot_token].add(summed, mode='drop')]
    reduce_sum x3, other arithmetic: 13.6 us -> 0.4 us  [the longest x1 0.36 us: local(): jnp.sum(jnp.where(mine[:, None, :] == slots[None, :, None], gain[:, None,...]
  transfers between devices with their start and end apart: 5 -> 0, of which waited for: 3 -> 0; matrix products, arithmetic and copies ran while one was open for 8% -> 0% of each run, Pallas kernels for 0% -> 0%
where the time goes in v1:
time: 275 us; the launch traced here: 273 us
  Pallas kernels  236 us (86%)
  blocking collectives  19.3 us (7%)
  local copies, waits for them, and re-layouts  12.9 us (5%)
  other arithmetic  4.09 us (1%)
    pallas_call x1, Pallas kernels, give_back(): pl.pallas_call(return_kernel, out_shape=(jax.ShapeDtypeStruct((TOK, D), B...  129 us
    pallas_call x1, Pallas kernels, dispatch(): pl.pallas_call(dispatch_kernel, out_shape=(jax.ShapeDtypeStruct((TOK, D),...  107 us
    all_gather x1, blocking collectives, local(): gathered = lax.all_gather(info, 'ep')  19.3 us
    unnamed x10, local copies, waits for them, and re-layouts  9.09 us

profile of v1, /device:TPU:7, one launch (start us, length us, event | category | flops | bytes accessed | tf_op | source)
XLA Modules:
  0.0 273.4 jit_solution(6118817782140751665)
XLA Ops:
  0.7 0.7 convert_bitcast_fusion
  1.3 0.7 iota_compare_fusion.5
  2.0 0.7 fusion.9
  2.7 0.1 eq.104
  2.8 19.3 %all-gather.1 = f32[16,4,128]{2,1,0:T(4,128)S(1)} all-gather(f32[1,4,128]{2,1,0:T(4,128)S(1)} %maximum_bitcast_fusion), channel_id=2, replica_groups=mesh['section'=8,'ep'=16] {'ep'}, dimensions={0}, use_global_device_ids=true | all-gather | bytes 34816 | tf_op jit(solution)/shard_map/all_gather | solution.py:512
  22.1 0.1 convolution_select_fusion
  22.3 0.4 select_reduce_fusion
  22.7 0.0 copy-start.3
  22.8 0.1 copy.40
  22.9 0.2 copy.41
  23.1 0.7 broadcast_select_fusion.spread_k
  23.9 0.1 fusion.pick
  23.9 0.9 eq.101
  24.8 1.3 copy.38
  26.2 0.8 compare_convert_fusion.spread
  27.0 1.1 copy.42.sw
  28.1 0.0 copy-done.3
  28.1 2.0 copy-done
  30.2 107.0 %dispatch.1 = (bf16[128,7168]{1,0:T(8,128)(2,1)S(1)}, bf16[4,4,4,80,256]{4,3,2,1,0:T(8,128)(2,1)S(1)}) custom-call(bf16[128,7168]{1,0:T(8,128)(2,1)S(1)} %bitcast.35, bf16[256,7168]{1,0:T(8,128)(2,1)S(1)} %bitcast.34, bf16[4,4,80,128]{3,2,1,0:T(8,128)(2,1)S(1)} %fusion.pick), custom_call_target="tpu_custom_call" | custom-call | tf_op jit(solution)/shard_map/dispatch/pallas_call | solution.py:443
  137.2 1.5 copy-done.1
  138.7 1.2 copy-done.2
  139.9 129.1 %give_back.1 = (bf16[128,7168]{1,0:T(8,128)(2,1)}, f32[128,2]{1,0:T(8,128)}) custom-call(bf16[4,4,4,80,256]{4,3,2,1,0:T(8,128)(2,1)} %copy-done.1, bf16[4,4,80,256]{3,2,1,0:T(8,128)(2,1)} %bitcast.40, bf16[4,4,80,256]{3,2,1,0:T(8,128)(2,1)} %bitcast.41, f32[4,4,80,1]{3,2,1,0:T(8,128)} %copy.42.sw, bf16[7168,256]{1,0:T(8,128)(2,1)} %bitcast.36, ...), custom_call_target="tpu_custom_call" | custom-call | tf_op jit(solution)/shard_map/give_back/pallas_call | solution.py:470
  269.1 1.5 copy.43
  270.5 2.8 %copy.45 = bf16[1,128,7168]{2,1,0:T(8,128)(2,1)} copy(bf16[1,128,7168]{2,1,0:T(8,128)(2,1)} %bitcast.39) | data formatting | bytes 3670016
  (16 shorter events, 0.2 us)
Async XLA Ops:
  22.7 5.5 %copy-start.3 = (bf16[1,128,7168]{2,1,0:T(8,128)(2,1)S(1)}, bf16[1,128,7168]{2,1,0:T(8,128)(2,1)}, u32[]{:S(2)}) copy-start(bf16[1,128,7168]{2,1,0:T(8,128)(2,1)} %param.8) | copy-start | bytes 5505028
  28.1 2.0 copy-start
  137.2 1.5 copy-start.1
  138.7 1.2 copy-start.2

commit v2 on v1

v2 whole, which is shorter than its diff:
```python
import jax
import jax.numpy as jnp
from jax import lax
from jax.experimental import pallas as pl
from jax.experimental.pallas import tpu as pltpu
from jax.sharding import PartitionSpec as P

MESH = pl.DeviceIdType.MESH
BF = jnp.bfloat16
F32 = jnp.float32

SECTIONS = 8
E_WIN = 4
SLICES = 4
TOPK = 2
CAP = 80
TOK = 128
D = 7168
HID = 256
Q = D // SLICES
ROWS = SLICES * CAP
NQ = 2
QH = Q // NQ

CW = 512
CA = 4096
NA = CA // CW
HA = NA // 2
NB = (D - CA) // CW
HB = NB // 2
RT = 128
WA = CA + RT
BCOL = WA
WB = D - CA


def dot_nt(a, b):
    return lax.dot_general(a, b, (((1,), (1,)), ((), ())), preferred_element_type=F32)


def place():
    s = lax.axis_index("section")
    p = lax.axis_index("ep")
    return s, p // SLICES, lax.rem(p, SLICES)


def shifted(a, by, n):
    return lax.rem(a + by + n, n)


def cols(start, width):
    return pl.ds(pl.multiple_of(start, 128), width)


def remote(src, dst, send, recv, device):
    return pltpu.make_async_remote_copy(
        src_ref=src, dst_ref=dst, send_sem=send, recv_sem=recv, device_id=device, device_id_type=MESH
    )


def layer_kernel(
    up, routes, gains, gate, upv, wg, wu, wd, out, router,
    info, slot_gain, pick, spread, gate_v, up_v, wdr, cot,
    grads, weights, partial, r1p, r1m, r2p, r2m, arecv, brecv, ctok, rb1p, rb1m, rb2p, rb2m,
    iz_s, iz_r, iy_s, iy_r, tok_s, tok_r, wd_s, wd_r, cot_s, cot_r, y_s, y_r, g_s, g_r, loc, out_s,
    w_sem, r1_s, r1_r, r2p_s, r2p_r, r2m_s, r2m_r, ay_s, ay_r, by_s, by_r, b1_s, b1_r, b2p_s, b2p_r, b2m_s, b2m_r,
):
    s, y, z = place()
    behind = shifted(s, -1, SECTIONS)
    ahead = shifted(s, 1, SECTIONS)
    zp, zm, z2 = shifted(z, 1, SLICES), shifted(z, -1, SLICES), shifted(z, 2, SLICES)

    def along_z(k):
        return (s, y * SLICES + shifted(z, k, SLICES))

    def along_y(k):
        return (s, shifted(y, k, E_WIN) * SLICES + z)

    right, left = along_z(1), along_z(3)

    barrier = pltpu.get_barrier_semaphore()
    for k in range(SLICES):
        pl.semaphore_signal(barrier, inc=1, device_id=(ahead, y * SLICES + k), device_id_type=MESH)
    for k in range(1, SLICES):
        pl.semaphore_signal(barrier, inc=1, device_id=along_z(k), device_id_type=MESH)
        pl.semaphore_signal(barrier, inc=1, device_id=along_y(k), device_id_type=MESH)

    def w_copy(c):
        take = pl.ds(c * CW, CW)
        return (
            pltpu.make_async_copy(wg.at[take], weights.at[c, :, pl.ds(0, HID)], w_sem.at[0, c]),
            pltpu.make_async_copy(wu.at[take], weights.at[c, :, pl.ds(HID, HID)], w_sem.at[1, c]),
        )

    wd_own = pltpu.make_async_copy(wd.at[:, cols(z * Q, Q)], wdr.at[z], loc.at[0])
    saved = (pltpu.make_async_copy(gate, gate_v, loc.at[1]), pltpu.make_async_copy(upv, up_v, loc.at[2]))

    info[y, z] = jnp.concatenate(
        [routes[...].astype(F32), gains[...].astype(F32), jnp.zeros((8 - 2 * TOPK, TOK), F32)], axis=0
    )
    row8 = lax.broadcasted_iota(jnp.int32, (8, TOK), 0).astype(F32)
    later = lax.broadcasted_iota(jnp.int32, (TOK, TOK), 1)
    earlier = lax.broadcasted_iota(jnp.int32, (TOK, TOK), 0)
    before = (earlier < later).astype(F32).astype(BF)
    unit = (earlier == later).astype(F32).astype(BF)
    slot_row = lax.broadcasted_iota(jnp.int32, (CAP, TOK), 0).astype(F32)

    pl.semaphore_wait(barrier, 10)

    def slots(k, m):
        return partial.at[k, m, :, pl.ds(0, Q)]

    def recv(owner, source):
        return partial.at[owner, source, :, pl.ds(Q, Q)]

    def ps(k, yb):
        return partial.at[yb, :, :, cols(2 * Q + (SLICES + k) * HID, HID)]

    def bp(owner, yb):
        return partial.at[yb, :, :, cols(2 * Q + owner * HID, HID)]

    def tok(source, h):
        return ctok.at[source, :, pl.ds(h * QH, QH)]

    def info_z(k, owner):
        return remote(info.at[y, z], info.at[y, owner], iz_s.at[k], iz_r.at[k], along_z(k))

    def info_y(k, owner):
        return remote(info.at[y], info.at[owner], iy_s.at[k], iy_r.at[k], along_y(k))

    def tok_copy(k, h, owner):
        q = shifted(z, k, SLICES)
        return remote(
            up.at[:, cols(q * Q + h * QH, QH)], tok(owner, h), tok_s.at[k, h], tok_r.at[k, h], (behind, y * SLICES + q)
        )

    def wd_copy(k, owner):
        q = shifted(z, k, SLICES)
        return remote(wd.at[:, cols(q * Q, Q)], wdr.at[owner], wd_s.at[k], wd_r.at[k], along_z(k))

    cot_copy = remote(up, cot, cot_s, cot_r, (behind, y * SLICES + z))

    def y_copy(k, m, h, source, owner):
        return remote(
            slots(k, m).at[:, pl.ds(h * QH, QH)],
            recv(owner, source).at[:, pl.ds(h * QH, QH)],
            y_s.at[k, m, h], y_r.at[k, m, h], along_y(k),
        )

    def g_copy(k, m, yb, owner):
        return remote(ps(k, yb), bp(owner, yb), g_s.at[k, m], g_r.at[k, m], along_z(k))

    for k in (2, 1, 3):
        info_z(k, z).start()
    for h in range(NQ):
        for k in (2, 1, 3, 0):
            tok_copy(k, h, z).start()
    wd_own.start()
    for copy in saved:
        copy.start()

    def start_weights(c, _):
        for copy in w_copy(c):
            copy.start()
        return 0

    lax.fori_loop(0, D // CW, start_weights, 0)

    for k in (1, 3, 2):
        info_z(k, shifted(z, -k, SLICES)).wait_recv()
    for k in (2, 1, 3):
        info_y(k, y).start()

    def slot_of(block):
        hit = (block[0:1] == row8) | (block[1:2] == row8)
        rank = jnp.dot(hit.astype(F32).astype(BF), before, preferred_element_type=F32)
        return jnp.where(hit, rank, -1.0)

    def row_tables(zz, _):
        slot = slot_of(info[y, zz])
        for e in range(E_WIN):
            pick[zz, e] = (slot_row == slot[e:e + 1]).astype(F32).astype(BF)
        spread[zz] = dot_nt(unit, pick[zz].reshape(E_WIN * CAP, TOK)).astype(BF)
        return 0

    lax.fori_loop(0, SLICES, row_tables, 0)

    order = (0, 1, 3, 2)
    for h in range(NQ):
        for m in order:
            source = shifted(z, -m, SLICES)
            tok_copy(m, h, source).wait_recv()
            if h == NQ - 1 and m == order[-1]:
                for k in (2, 1, 3):
                    wd_copy(k, z).start()
                cot_copy.start()

            def pack(k, _):
                e = shifted(y, k, E_WIN)
                rows = jnp.dot(pick[source, e], tok(source, h)[...], preferred_element_type=F32).astype(BF)
                slots(k, m).at[:, pl.ds(h * QH, QH)][...] = rows
                y_copy(k, m, h, source, y).start()
                return 0

            lax.fori_loop(1, E_WIN, pack, 0)
            rows = jnp.dot(pick[source, y], tok(source, h)[...], preferred_element_type=F32).astype(BF)
            recv(y, source).at[:, pl.ds(h * QH, QH)][...] = rows

    for k in (1, 3, 2):
        info_y(k, shifted(y, -k, E_WIN)).wait_recv()

    def expert_tables(i, _):
        b, zz = i // SLICES, lax.rem(i, SLICES)
        block = info[b, zz]
        here = y.astype(F32)
        slot = jnp.sum(jnp.where(row8 == here, slot_of(block), 0.0), axis=0, keepdims=True)
        gain = jnp.where(block[0:1] == here, block[2:3], 0.0) + jnp.where(block[1:2] == here, block[3:4], 0.0)
        slot_gain[b, zz, pl.ds(0, 1)] = slot
        slot_gain[b, zz, pl.ds(1, 1)] = gain
        return 0

    lax.fori_loop(0, E_WIN * SLICES, expert_tables, 0)

    wd_own.wait()
    for k in (1, 3, 2):
        wd_copy(k, shifted(z, -k, SLICES)).wait_recv()

    own = []
    for m in (0, 1, 3, 2):
        yb = shifted(y, -m, E_WIN)
        if m:
            for h in range(NQ):
                for j in order:
                    y_copy(m, j, h, shifted(z, -j, SLICES), yb).wait_recv()

        def rows_of():
            return partial[yb, :, :, pl.ds(Q, Q)].reshape(ROWS, Q)

        def partial_grad(k, _):
            part = dot_nt(rows_of(), wdr[shifted(z, k, SLICES)])
            ps(k, yb)[...] = part.astype(BF).reshape(SLICES, CAP, HID)
            g_copy(k, m, yb, z).start()
            return 0

        lax.fori_loop(1, SLICES, partial_grad, 0)
        bp(z, yb)[...] = dot_nt(rows_of(), wdr[z]).astype(BF).reshape(SLICES, CAP, HID)

    for copy in saved:
        copy.wait()

    for m in (0, 1, 3, 2):
        yb = shifted(y, -m, E_WIN)
        for k in (1, 3, 2):
            g_copy(k, m, yb, shifted(z, -k, SLICES)).wait_recv()

        def elementwise(zz, _):
            back = partial[yb, zz, :, pl.ds(2 * Q, HID)].astype(F32)
            for k in range(1, SLICES):
                back = back + partial[yb, zz, :, pl.ds(2 * Q + k * HID, HID)].astype(F32)
            g = gate_v[yb * SLICES + zz].astype(F32)
            u = up_v[yb * SLICES + zz].astype(F32)
            held = slot_row == slot_gain[yb, zz, pl.ds(0, 1)]
            gain = jnp.sum(jnp.where(held, slot_gain[yb, zz, pl.ds(1, 1)], 0.0), axis=-1, keepdims=True)
            sig = 1.0 / (1.0 + jnp.exp(-g))
            silu = g * sig
            part = jnp.sum(silu * u * back, axis=-1, keepdims=True)
            lane = lax.broadcasted_iota(jnp.int32, (CAP, RT), 1)
            partial[yb, zz, :, pl.ds(CA, RT)] = jnp.where(lane == z, part, 0.0).astype(BF)
            scaled = back * gain
            grads[yb, zz, :, pl.ds(0, HID)] = (scaled * u * sig * (1.0 + g * (1.0 - sig))).astype(BF)
            grads[yb, zz, :, pl.ds(HID, HID)] = (scaled * silu).astype(BF)
            return 0

        lax.fori_loop(0, SLICES, elementwise, 0)

    for k in range(1, SLICES):
        for m in range(SLICES):
            for h in range(NQ):
                y_copy(k, m, h, shifted(z, -m, SLICES), y).wait_send()
            g_copy(k, m, shifted(y, -m, E_WIN), z).wait_send()

    def first(half, col, width, i):
        src = partial.at[:, z2, :, cols(col, width)]
        if half == 0:
            return remote(src, r1p.at[:, :, cols(col, width)], r1_s.at[i], r1_r.at[i], right)
        return remote(src, r1m.at[:, :, cols(col - CA // 2, width)], r1_s.at[i], r1_r.at[i], left)

    def to_right(col, width, i):
        src = partial.at[:, zp, :, cols(col, width)]
        return remote(src, r2p.at[:, :, cols(col, width)], r2p_s.at[i], r2p_r.at[i], right)

    def to_left(col, width, i):
        src = partial.at[:, zm, :, cols(col, width)]
        return remote(src, r2m.at[:, :, cols(col, width)], r2m_s.at[i], r2m_r.at[i], left)

    def a_copy(k, col, width, i):
        src = partial.at[shifted(y, k, E_WIN), z, :, cols(col, width)]
        return remote(src, arecv.at[y, :, cols(col, width)], ay_s.at[k, i], ay_r.at[k, i], along_y(k))

    def b_copy(k, j):
        src = partial.at[shifted(y, k, E_WIN), :, :, cols(BCOL + j * CW, CW)]
        return remote(src, brecv.at[:, y, :, cols(j * CW, CW)], by_s.at[k, j], by_r.at[k, j], along_y(k))

    def b_first(half, j):
        src = ctok.at[z2, :, cols(j * CW, CW)]
        if half == 0:
            return remote(src, rb1p.at[:, cols(j * CW, CW)], b1_s.at[j], b1_r.at[j], right)
        return remote(src, rb1m.at[:, cols((j - HB) * CW, CW)], b1_s.at[j], b1_r.at[j], left)

    def b_right(j):
        return remote(ctok.at[zp, :, cols(j * CW, CW)], rb2p.at[:, cols(j * CW, CW)], b2p_s.at[j], b2p_r.at[j], right)

    def b_left(j):
        return remote(ctok.at[zm, :, cols(j * CW, CW)], rb2m.at[:, cols(j * CW, CW)], b2m_s.at[j], b2m_r.at[j], left)

    first(1, CA, RT, NA).start()
    to_right(CA, RT, NA).start()

    def input_part(c, col):
        for copy in w_copy(c):
            copy.wait()

        def block(b, _):
            part = dot_nt(grads[b].reshape(ROWS, 2 * HID), weights[c])
            partial[b, :, :, cols(col, CW)] = part.astype(BF).reshape(SLICES, CAP, CW)
            return 0

        lax.fori_loop(0, E_WIN, block, 0)

    def produce_a(c, half):
        input_part(c, c * CW)
        first(half, c * CW, CW, c).start()
        if half == 0:
            to_left(c * CW, CW, c).start()
        else:
            to_right(c * CW, CW, c).start()

    def produce_b(j):
        input_part(NA + j, BCOL + j * CW)
        for k in (2, 1, 3):
            b_copy(k, j).start()
        brecv[:, y, :, cols(j * CW, CW)] = partial[y, :, :, cols(BCOL + j * CW, CW)]

    def produce(i, _):
        produce_a(i, 0)
        produce_a(HA + i, 1)
        produce_b(i)
        return 0

    lax.fori_loop(0, HA, produce, 0)

    def produce_rest(j, _):
        produce_b(j)
        return 0

    lax.fori_loop(HA, NB, produce_rest, 0)

    def relay(half, col, width, i):
        first(half, col, width, i).wait_recv()
        if half == 0:
            mine, other = partial.at[:, zp, :, cols(col, width)], r1p.at[:, :, cols(col, width)]
        else:
            mine, other = partial.at[:, zm, :, cols(col, width)], r1m.at[:, :, cols(col - CA // 2, width)]
        mine[...] = (mine[...].astype(F32) + other[...].astype(F32)).astype(BF)
        if half == 0:
            to_right(col, width, i).start()
        else:
            to_left(col, width, i).start()

    relay(1, CA, RT, NA)

    def relay_pair(i, _):
        relay(0, i * CW, CW, i)
        relay(1, (HA + i) * CW, CW, HA + i)
        return 0

    lax.fori_loop(0, HA, relay_pair, 0)

    def finish_a(col, width, i):
        to_right(col, width, i).wait_recv()
        to_left(col, width, i).wait_recv()
        mine = partial.at[:, z, :, cols(col, width)]
        total = mine[...].astype(F32) + r2p[:, :, cols(col, width)].astype(F32) + r2m[:, :, cols(col, width)].astype(F32)
        mine[...] = total.astype(BF)
        for k in (2, 1, 3):
            a_copy(k, col, width, i).start()
        arecv[y, :, cols(col, width)] = partial[y, z, :, cols(col, width)]

    def tokens_b(half, j):
        for k in (1, 3, 2):
            b_copy(k, j).wait_recv()

        def combine(zz, _):
            rows = brecv[zz, :, :, cols(j * CW, CW)].reshape(E_WIN * CAP, CW)
            ctok[zz, :, cols(j * CW, CW)] = jnp.dot(spread[zz], rows, preferred_element_type=F32).astype(BF)
            return 0

        lax.fori_loop(0, SLICES, combine, 0)
        b_first(half, j).start()
        if half == 0:
            b_left(j).start()
        else:
            b_right(j).start()

    finish_a(CA, RT, NA)

    def second(i, _):
        tokens_b(0, i)
        finish_a(i * CW, CW, i)
        tokens_b(1, HB + i)
        finish_a((HA + i) * CW, CW, HA + i)
        return 0

    lax.fori_loop(0, HB, second, 0)
    for i in range(HB, HA):
        finish_a(i * CW, CW, i)
        finish_a((HA + i) * CW, CW, HA + i)

    def relay_b(half, j):
        b_first(half, j).wait_recv()
        if half == 0:
            mine, other = ctok.at[zp, :, cols(j * CW, CW)], rb1p.at[:, cols(j * CW, CW)]
        else:
            mine, other = ctok.at[zm, :, cols(j * CW, CW)], rb1m.at[:, cols((j - HB) * CW, CW)]
        mine[...] = (mine[...].astype(F32) + other[...].astype(F32)).astype(BF)
        if half == 0:
            b_right(j).start()
        else:
            b_left(j).start()

    def relay_b_pair(i, _):
        relay_b(0, i)
        relay_b(1, HB + i)
        return 0

    lax.fori_loop(0, HB, relay_b_pair, 0)

    for k in range(1, E_WIN):
        a_copy(k, CA, RT, NA).wait_recv()
    parts = dot_nt(unit, arecv[:, :, pl.ds(CA, RT)].reshape(E_WIN * CAP, RT)).astype(BF)
    expert = lax.broadcasted_iota(jnp.int32, (E_WIN, CAP, TOK), 0)
    for k in range(TOPK):
        chosen = jnp.where(expert == routes[pl.ds(k, 1)].reshape(1, 1, TOK), pick[z].astype(F32), 0.0).astype(BF)
        values = jnp.dot(parts, chosen.reshape(E_WIN * CAP, TOK), preferred_element_type=F32)
        router[pl.ds(k, 1)] = jnp.sum(values, axis=0, keepdims=True)

    def out_copy(c):
        return pltpu.make_async_copy(cot.at[:, cols(c * CW, CW)], out.at[:, cols(c * CW, CW)], out_s.at[c])

    cot_copy.wait_recv()

    def last_a(c, _):
        for k in (1, 3, 2):
            a_copy(k, c * CW, CW, c).wait_recv()
        rows = arecv[:, :, cols(c * CW, CW)].reshape(E_WIN * CAP, CW)
        total = jnp.dot(spread[z], rows, preferred_element_type=F32)
        cot[:, cols(c * CW, CW)] = (cot[:, cols(c * CW, CW)].astype(F32) + total).astype(BF)
        out_copy(c).start()
        return 0

    lax.fori_loop(0, NA, last_a, 0)

    def last_b(j, _):
        b_right(j).wait_recv()
        b_left(j).wait_recv()
        take = cols(j * CW, CW)
        total = ctok[z, :, take].astype(F32) + rb2p[:, take].astype(F32) + rb2m[:, take].astype(F32)
        cot[:, cols(CA + j * CW, CW)] = (cot[:, cols(CA + j * CW, CW)].astype(F32) + total).astype(BF)
        out_copy(NA + j).start()
        return 0

    lax.fori_loop(0, NB, last_b, 0)

    def sent_a(half, col, width, i):
        first(half, col, width, i).wait_send()
        to_right(col, width, i).wait_send()
        to_left(col, width, i).wait_send()
        for k in range(1, E_WIN):
            a_copy(k, col, width, i).wait_send()

    def sent_a_pair(i, _):
        sent_a(0, i * CW, CW, i)
        sent_a(1, (HA + i) * CW, CW, HA + i)
        return 0

    lax.fori_loop(0, HA, sent_a_pair, 0)
    sent_a(1, CA, RT, NA)

    def sent_b(half, j):
        for k in range(1, E_WIN):
            b_copy(k, j).wait_send()
        b_first(half, j).wait_send()
        b_right(j).wait_send()
        b_left(j).wait_send()

    def sent_b_pair(i, _):
        sent_b(0, i)
        sent_b(1, HB + i)
        return 0

    lax.fori_loop(0, HB, sent_b_pair, 0)

    def written(c, _):
        out_copy(c).wait()
        return 0

    lax.fori_loop(0, D // CW, written, 0)

    cot_copy.wait_send()
    for k in range(1, SLICES):
        info_z(k, z).wait_send()
        info_y(k, y).wait_send()
        wd_copy(k, z).wait_send()
    for h in range(NQ):
        for k in range(SLICES):
            tok_copy(k, h, z).wait_send()


def vmem(*shape, dtype=BF):
    return pltpu.VMEM(shape, dtype)


def sems(*shape):
    return pltpu.SemaphoreType.DMA(shape)


ANY = pl.BlockSpec(memory_space=pl.ANY)
VM = pl.BlockSpec(memory_space=pltpu.VMEM)


def layer(upstream, routes, gains, gate, up, w_gate, w_up, w_down):
    return pl.pallas_call(
        layer_kernel,
        out_shape=(
            jax.ShapeDtypeStruct((TOK, D), BF),
            jax.ShapeDtypeStruct((TOPK, TOK), F32),
        ),
        in_specs=[ANY, VM, VM, ANY, ANY, ANY, ANY, ANY],
        out_specs=(ANY, VM),
        scratch_shapes=[
            vmem(E_WIN, SLICES, 8, TOK, dtype=F32),
            vmem(E_WIN, SLICES, 8, TOK, dtype=F32),
            vmem(SLICES, E_WIN, CAP, TOK),
            vmem(SLICES, TOK, E_WIN * CAP),
            vmem(E_WIN * SLICES, CAP, HID),
            vmem(E_WIN * SLICES, CAP, HID),
            vmem(SLICES, HID, Q),
            vmem(TOK, D),
            vmem(E_WIN, SLICES, CAP, 2 * HID),
            vmem(D // CW, CW, 2 * HID),
            vmem(E_WIN, SLICES, CAP, D + RT),
            vmem(E_WIN, CAP, CA // 2),
            vmem(E_WIN, CAP, CA // 2 + RT),
            vmem(E_WIN, CAP, WA),
            vmem(E_WIN, CAP, WA),
            vmem(E_WIN, CAP, WA),
            vmem(SLICES, E_WIN, CAP, WB),
            vmem(SLICES, TOK, WB),
            vmem(TOK, WB // 2),
            vmem(TOK, WB // 2),
            vmem(TOK, WB),
            vmem(TOK, WB),
            sems(SLICES), sems(SLICES),
            sems(E_WIN), sems(E_WIN),
            sems(SLICES, NQ), sems(SLICES, NQ),
            sems(SLICES), sems(SLICES),
            pltpu.SemaphoreType.DMA, pltpu.SemaphoreType.DMA,
            sems(E_WIN, SLICES, NQ), sems(E_WIN, SLICES, NQ),
            sems(SLICES, E_WIN), sems(SLICES, E_WIN),
            sems(3),
            sems(D // CW),
            sems(2, D // CW),
            sems(NA + 1), sems(NA + 1),
            sems(NA + 1), sems(NA + 1),
            sems(NA + 1), sems(NA + 1),
            sems(E_WIN, NA + 1), sems(E_WIN, NA + 1),
            sems(E_WIN, NB), sems(E_WIN, NB),
            sems(NB), sems(NB),
            sems(NB), sems(NB),
            sems(NB), sems(NB),
        ],
        compiler_params=pltpu.CompilerParams(collective_id=0, has_side_effects=True, vmem_limit_bytes=63 * 2**20),
        name="layer",
    )(upstream, routes, gains, gate, up, w_gate, w_up, w_down)


def local(upstream, routes, combine_weights, gate_saved, up_saved, w_gate, w_up, w_down):
    grad_input, router_grad = layer(
        upstream[0], routes[0].T, combine_weights[0].T, gate_saved[0], up_saved[0], w_gate[0], w_up[0], w_down[0]
    )
    return grad_input[None], router_grad.T[None]


def solution(mesh):
    in_specs = (
        P("section", "ep", None),
        P("section", "ep", None),
        P("section", "ep", None),
        P("section", None, None, "ep"),
        P("section", None, None, "ep"),
        P("section", None, "ep"),
        P("section", None, "ep"),
        P("section", "ep", None),
    )
    out_specs = (P("section", "ep", None), P("section", "ep", None))
    return jax.shard_map(local, mesh=mesh, in_specs=in_specs, out_specs=out_specs, check_vma=False)
```

time: 275 us -> 234 us (0.85)
  blocking collectives: 19.3 us -> 0 us
  local copies, waits for them, and re-layouts: 12.9 us -> 3.41 us
  Pallas kernels: 236 us -> 229 us
  other arithmetic: 4.09 us -> 0 us
    all_gather x1 -> x0, blocking collectives: 19.3 us -> none  [local(): gathered = lax.all_gather(info, 'ep')]
    pallas_call x2 -> x1, Pallas kernels: 236 us -> 229 us  [layer(): pl.pallas_call(layer_kernel, out_shape=(jax.ShapeDtypeStruct((TOK, D), BF...]
    unnamed x10 -> x4, local copies, waits for them, and re-layouts: 9.09 us -> 3.41 us
where the time goes in v2:
time: 234 us; the launch traced here: 233 us
  Pallas kernels  229 us (98%)
  local copies, waits for them, and re-layouts  3.41 us (1%)
    pallas_call x1, Pallas kernels, layer(): pl.pallas_call(layer_kernel, out_shape=(jax.ShapeDtypeStruct((TOK, D), BF...  229 us

profile of v2, /device:TPU:7, one launch (start us, length us, event | category | flops | bytes accessed | tf_op | source)
XLA Modules:
  0.0 233.3 jit_solution(944985910274884794)
XLA Ops:
  0.6 229.2 %layer.1 = (bf16[128,7168]{1,0:T(8,128)(2,1)}, f32[2,128]{1,0:T(2,128)}) custom-call(bf16[128,7168]{1,0:T(8,128)(2,1)} %bitcast.20, s32[2,128]{1,0:T(2,128)} %bitcast.23, bf16[2,128]{1,0:T(2,128)(2,1)} %bitcast.25, bf16[16,80,256]{2,1,0:T(8,128)(2,1)} %bitcast.21, bf16[16,80,256]{2,1,0:T(8,128)(2,1)} %bitcast.22, bf16[7168,256]{1,0:T(8,128)(2,1)} %bitcast.16, ...), custom_call_target="tpu_custom_call" | custom-call | tf_op jit(solution)/shard_map/layer/pallas_call | solution.py:532
  229.8 0.0 copy-start
  229.8 2.8 %copy.12 = bf16[1,128,7168]{2,1,0:T(8,128)(2,1)} copy(bf16[1,128,7168]{2,1,0:T(8,128)(2,1)} %bitcast.19) | data formatting | bytes 3670016
  232.7 0.0 copy-done
  232.7 0.6 copy.13
Async XLA Ops:
  229.8 2.9 %copy-start = (f32[2,128]{1,0:T(2,128)S(1)}, f32[2,128]{1,0:T(2,128)}, u32[]{:S(2)}) copy-start(f32[2,128]{1,0:T(2,128)} %get-tuple-element.5) | copy-start | bytes 3076

commit v3 on v2

v3 whole, which is shorter than its diff:
```python
import jax
import jax.numpy as jnp
from jax import lax
from jax.experimental import pallas as pl
from jax.experimental.pallas import tpu as pltpu
from jax.sharding import PartitionSpec as P

MESH = pl.DeviceIdType.MESH
BF = jnp.bfloat16
F32 = jnp.float32

SECTIONS = 8
E_WIN = 4
SLICES = 4
TOPK = 2
CAP = 80
TOK = 128
D = 7168
HID = 256
Q = D // SLICES
ROWS = SLICES * CAP
NQ = 7
QH = Q // NQ
FLY = 3

CW = 512
CA = 4096
NA = CA // CW
HA = NA // 2
HALF = CA // 2
WB = D - CA
NB = WB // CW
HB = NB // 2
HALFB = WB // 2
BLOCKS = (0, 1, 3, 2)


def dot_nt(a, b):
    return lax.dot_general(a, b, (((1,), (1,)), ((), ())), preferred_element_type=F32)


def place():
    s = lax.axis_index("section")
    p = lax.axis_index("ep")
    return s, p // SLICES, lax.rem(p, SLICES)


def shifted(a, by, n):
    return lax.rem(a + by + n, n)


def cols(start, width):
    return pl.ds(pl.multiple_of(start, 128), width)


def remote(src, dst, send, recv, device):
    return pltpu.make_async_remote_copy(
        src_ref=src, dst_ref=dst, send_sem=send, recv_sem=recv, device_id=device, device_id_type=MESH
    )


def layer_kernel(
    up, routes, gains, gate, upv, wg, wu, wd, out, router,
    info, slot_gain, pick, spread, gate_v, up_v, wdr, cot, parts, parts_sum, parts_in,
    grads, weights, partial, r1p, r1m, r2p, r2m, arecv, brecv, ctok, rb1p, rb1m, rb2p, rb2m,
    iz_s, iz_r, iy_s, iy_r, tok_s, tok_r, wd_s, wd_r, cot_s, cot_r, y_s, y_r,
    g1_s, g1_r, g2_s, g2_r, loc, out_s, pz_s, pz_r, py_s, py_r,
    w_sem, r1_s, r1_r, r2p_s, r2p_r, r2m_s, r2m_r, ay_s, ay_r, by_s, by_r, b1_s, b1_r, b2p_s, b2p_r, b2m_s, b2m_r,
):
    s, y, z = place()
    behind = shifted(s, -1, SECTIONS)
    ahead = shifted(s, 1, SECTIONS)
    zp, zm, z2 = shifted(z, 1, SLICES), shifted(z, -1, SLICES), shifted(z, 2, SLICES)

    def along_z(k):
        return (s, y * SLICES + shifted(z, k, SLICES))

    def along_y(k):
        return (s, shifted(y, k, E_WIN) * SLICES + z)

    right, left = along_z(1), along_z(3)

    barrier = pltpu.get_barrier_semaphore()
    for k in range(SLICES):
        pl.semaphore_signal(barrier, inc=1, device_id=(ahead, y * SLICES + k), device_id_type=MESH)
    for k in range(1, SLICES):
        pl.semaphore_signal(barrier, inc=1, device_id=along_z(k), device_id_type=MESH)
        pl.semaphore_signal(barrier, inc=1, device_id=along_y(k), device_id_type=MESH)

    def w_copy(c):
        take = pl.ds(c * CW, CW)
        return (
            pltpu.make_async_copy(wg.at[take], weights.at[c, :, pl.ds(0, HID)], w_sem.at[0, c]),
            pltpu.make_async_copy(wu.at[take], weights.at[c, :, pl.ds(HID, HID)], w_sem.at[1, c]),
        )

    wd_own = pltpu.make_async_copy(wd.at[:, cols(z * Q, Q)], wdr.at[z], loc.at[0])
    saved = (pltpu.make_async_copy(gate, gate_v, loc.at[1]), pltpu.make_async_copy(upv, up_v, loc.at[2]))

    info[y, z] = jnp.concatenate(
        [routes[...].astype(F32), gains[...].astype(F32), jnp.zeros((8 - 2 * TOPK, TOK), F32)], axis=0
    )
    parts[z] = jnp.zeros((E_WIN, 8, TOK), F32)
    row8 = lax.broadcasted_iota(jnp.int32, (8, TOK), 0).astype(F32)
    later = lax.broadcasted_iota(jnp.int32, (TOK, TOK), 1)
    earlier = lax.broadcasted_iota(jnp.int32, (TOK, TOK), 0)
    before = (earlier < later).astype(F32).astype(BF)
    unit = (earlier == later).astype(F32).astype(BF)
    slot_row = lax.broadcasted_iota(jnp.int32, (CAP, TOK), 0).astype(F32)
    lane_row = lax.broadcasted_iota(jnp.int32, (CAP, TOK), 1).astype(F32)

    pl.semaphore_wait(barrier, 10)

    def slots(e):
        return partial.at[e, :, :, pl.ds(0, Q)]

    def recv(owner):
        return partial.at[owner, :, :, pl.ds(Q, Q)]

    def back(n, yb):
        return partial.at[yb, :, :, pl.ds(2 * Q + n * HID, HID)]

    def ps(k, yb):
        return partial.at[yb, :, :, pl.ds(2 * Q + (2 + k) * HID, HID)]

    def g1(half, yb):
        return partial.at[yb, :, :, pl.ds(2 * Q + 6 * HID + half * (HID // 2), HID // 2)]

    def piece(ref, half):
        return ref.at[:, :, pl.ds(half * (HID // 2), HID // 2)]

    def tok(source, h):
        return ctok.at[source, :, cols(h * QH, QH)]

    def info_z(k, owner):
        return remote(info.at[y, z], info.at[y, owner], iz_s.at[k], iz_r.at[k], along_z(k))

    def info_y(k, owner):
        return remote(info.at[y], info.at[owner], iy_s.at[k], iy_r.at[k], along_y(k))

    def tok_copy(k, h, owner):
        q = shifted(z, k, SLICES)
        return remote(
            up.at[:, cols(q * Q + h * QH, QH)], tok(owner, h), tok_s.at[k, h], tok_r.at[k, h], (behind, y * SLICES + q)
        )

    def wd_copy(k, owner):
        q = shifted(z, k, SLICES)
        return remote(wd.at[:, cols(q * Q, Q)], wdr.at[owner], wd_s.at[k], wd_r.at[k], along_z(k))

    cot_copy = remote(up, cot, cot_s, cot_r, (behind, y * SLICES + z))

    def y_copy(k, h, owner):
        take = cols(h * QH, QH)
        return remote(
            slots(shifted(y, k, E_WIN)).at[:, :, take], recv(owner).at[:, :, take], y_s.at[k, h], y_r.at[k, h], along_y(k)
        )

    def g_first(half, m, yb):
        return remote(
            piece(ps(2, yb), half), g1(half, yb), g1_s.at[half, m], g1_r.at[half, m], (right, left)[half]
        )

    def g_second(side, half, m, yb):
        src = piece(ps((1, 3)[side], yb), half)
        return remote(
            src, piece(back(side, yb), half), g2_s.at[side, half, m], g2_r.at[side, half, m], (right, left)[side]
        )

    for k in (2, 1, 3):
        info_z(k, z).start()
    for h in range(FLY):
        for k in (2, 1, 3, 0):
            tok_copy(k, h, z).start()
    wd_own.start()
    for copy in saved:
        copy.start()

    def start_weights(c, _):
        for copy in w_copy(c):
            copy.start()
        return 0

    lax.fori_loop(0, D // CW, start_weights, 0)

    for k in (1, 3, 2):
        info_z(k, shifted(z, -k, SLICES)).wait_recv()
    for k in (2, 1, 3):
        info_y(k, y).start()

    def slot_of(block):
        hit = (block[0:1] == row8) | (block[1:2] == row8)
        rank = jnp.dot(hit.astype(F32).astype(BF), before, preferred_element_type=F32)
        return jnp.where(hit, rank, -1.0)

    def row_tables(zz, _):
        slot = slot_of(info[y, zz])
        for e in range(E_WIN):
            pick[zz, e] = (slot_row == slot[e:e + 1]).astype(F32).astype(BF)
        return 0

    lax.fori_loop(0, SLICES, row_tables, 0)

    def send_on(h):
        for k in range(SLICES):
            tok_copy(k, h, z).wait_send()
        for k in (2, 1, 3, 0):
            tok_copy(k, h + FLY, z).start()

    def pack(h):
        for k in (0, 1, 3, 2):
            tok_copy(k, h, shifted(z, -k, SLICES)).wait_recv()

        def pack_source(zz, _):
            rows = jnp.dot(pick[zz].reshape(E_WIN * CAP, TOK), tok(zz, h)[...], preferred_element_type=F32)
            partial[:, zz, :, cols(h * QH, QH)] = rows.astype(BF).reshape(E_WIN, CAP, QH)
            return 0

        lax.fori_loop(0, SLICES, pack_source, 0)
        for k in (1, 3, 2):
            y_copy(k, h, y).start()

    def dispatch(h, _):
        send_on(h)
        pack(h)
        return 0

    lax.fori_loop(0, NQ - FLY, dispatch, 0)
    for k in (2, 1, 3):
        wd_copy(k, z).start()
    cot_copy.start()

    def dispatch_rest(h, _):
        pack(h)
        return 0

    lax.fori_loop(NQ - FLY, NQ, dispatch_rest, 0)

    for k in (1, 3, 2):
        info_y(k, shifted(y, -k, E_WIN)).wait_recv()

    def expert_tables(i, _):
        b, zz = i // SLICES, lax.rem(i, SLICES)
        block = info[b, zz]
        here = y.astype(F32)
        slot = jnp.sum(jnp.where(row8 == here, slot_of(block), 0.0), axis=0, keepdims=True)
        gain = jnp.where(block[0:1] == here, block[2:3], 0.0) + jnp.where(block[1:2] == here, block[3:4], 0.0)
        slot_gain[b, zz, pl.ds(0, 1)] = slot
        slot_gain[b, zz, pl.ds(1, 1)] = gain
        return 0

    lax.fori_loop(0, E_WIN * SLICES, expert_tables, 0)

    def spread_tables(zz, _):
        spread[zz] = dot_nt(unit, pick[zz].reshape(E_WIN * CAP, TOK)).astype(BF)
        return 0

    lax.fori_loop(0, SLICES, spread_tables, 0)

    def block_of(m):
        return shifted(y, -m, E_WIN)

    def partial_grad(m):
        yb = block_of(m)
        if m:
            for h in range(NQ):
                y_copy(m, h, yb).wait_recv()

        def product(k):
            rows = (recv(yb) if m else slots(y))[...].reshape(ROWS, Q)
            return dot_nt(rows, wdr[shifted(z, k, SLICES)]).astype(BF).reshape(SLICES, CAP, HID)

        ps(2, yb)[...] = product(2)
        g_first(0, m, yb).start()
        g_first(1, m, yb).start()
        ps(1, yb)[...] = product(1)
        g_second(0, 1, m, yb).start()
        ps(3, yb)[...] = product(3)
        g_second(1, 0, m, yb).start()
        back(2, yb)[...] = product(0)

    def relay_grad(m):
        yb = block_of(m)
        for side in (0, 1):
            g_first(side, m, yb).wait_recv()
            mine = piece(ps((1, 3)[side], yb), side)
            mine[...] = (mine[...].astype(F32) + g1(side, yb)[...].astype(F32)).astype(BF)
            g_second(side, side, m, yb).start()

    def elementwise(m):
        yb = block_of(m)
        for side in (0, 1):
            for half in (0, 1):
                g_second(side, half, m, yb).wait_recv()

        def one(zz, _):
            total = back(0, yb)[zz].astype(F32) + back(1, yb)[zz].astype(F32) + back(2, yb)[zz].astype(F32)
            g = gate_v[yb * SLICES + zz].astype(F32)
            u = up_v[yb * SLICES + zz].astype(F32)
            held = slot_row == slot_gain[yb, zz, pl.ds(0, 1)]
            gain = jnp.sum(jnp.where(held, slot_gain[yb, zz, pl.ds(1, 1)], 0.0), axis=-1, keepdims=True)
            sig = 1.0 / (1.0 + jnp.exp(-g))
            silu = g * sig
            part = jnp.sum(silu * u * total, axis=-1, keepdims=True).astype(BF).astype(F32)
            parts[z, yb, pl.ds(zz, 1)] = jnp.sum(jnp.where(slot_row == lane_row, part, 0.0), axis=0, keepdims=True)
            scaled = total * gain
            grads[yb, zz, :, pl.ds(0, HID)] = (scaled * u * sig * (1.0 + g * (1.0 - sig))).astype(BF)
            grads[yb, zz, :, pl.ds(HID, HID)] = (scaled * silu).astype(BF)
            return 0

        lax.fori_loop(0, SLICES, one, 0)
        for half in (0, 1):
            g_first(half, m, yb).wait_send()
            for side in (0, 1):
                g_second(side, half, m, yb).wait_send()
        if m:
            for h in range(NQ):
                y_copy((E_WIN - m) % E_WIN, h, y).wait_send()

    def first(half, m, yb):
        src = partial.at[yb, z2, :, pl.ds(half * HALF, HALF)]
        return remote(src, (r1p, r1m)[half].at[yb], r1_s.at[half, m], r1_r.at[half, m], (right, left)[half])

    def to_right(half, m, yb):
        take = pl.ds(half * HALF, HALF)
        return remote(partial.at[yb, zp, :, take], r2p.at[yb, :, take], r2p_s.at[half, m], r2p_r.at[half, m], right)

    def to_left(half, m, yb):
        take = pl.ds(half * HALF, HALF)
        return remote(partial.at[yb, zm, :, take], r2m.at[yb, :, take], r2m_s.at[half, m], r2m_r.at[half, m], left)

    def a_copy(half, m, yb, owner):
        take = pl.ds(half * HALF, HALF)
        return remote(
            partial.at[yb, z, :, take], arecv.at[owner, :, take], ay_s.at[half, m], ay_r.at[half, m], along_y(-m)
        )

    def b_copy(half, m, yb, owner):
        return remote(
            partial.at[yb, :, :, pl.ds(CA + half * HALFB, HALFB)],
            brecv.at[:, owner, :, pl.ds(half * HALFB, HALFB)],
            by_s.at[half, m], by_r.at[half, m], along_y(-m),
        )

    def chunks_of(m, start, stop):
        yb = block_of(m)

        def chunk(c, _):
            part = dot_nt(grads[yb].reshape(ROWS, 2 * HID), weights[c])
            partial[yb, :, :, cols(c * CW, CW)] = part.astype(BF).reshape(SLICES, CAP, CW)
            return 0

        lax.fori_loop(start, stop, chunk, 0)
        return yb

    def input_a(m):
        yb = chunks_of(m, 0, HA)
        first(0, m, yb).start()
        to_left(0, m, yb).start()
        chunks_of(m, HA, NA)
        first(1, m, yb).start()
        to_right(1, m, yb).start()

    def input_b(m):
        for half in (0, 1):
            yb = chunks_of(m, NA + half * HB, NA + (half + 1) * HB)
            if m:
                b_copy(half, m, yb, y).start()
        if m == 0:

            def keep(zz, _):
                brecv[zz, y] = partial[y, zz, :, pl.ds(CA, WB)]
                return 0

            lax.fori_loop(0, SLICES, keep, 0)

    def relay(m):
        yb = block_of(m)
        for half in (0, 1):
            first(half, m, yb).wait_recv()

            def add(c, _):
                mine = partial.at[yb, (zp, zm)[half], :, cols(half * HALF + c * CW, CW)]
                other = (r1p, r1m)[half][yb, :, cols(c * CW, CW)]
                mine[...] = (mine[...].astype(F32) + other.astype(F32)).astype(BF)
                return 0

            lax.fori_loop(0, HA, add, 0)
            (to_right, to_left)[half](half, m, yb).start()

    def finish(m):
        yb = block_of(m)
        for half in (0, 1):
            to_right(half, m, yb).wait_recv()
            to_left(half, m, yb).wait_recv()

            def add(c, _):
                take = cols(half * HALF + c * CW, CW)
                mine = partial.at[yb, z, :, take]
                total = mine[...].astype(F32) + r2p[yb, :, take].astype(F32) + r2m[yb, :, take].astype(F32)
                if m:
                    mine[...] = total.astype(BF)
                else:
                    arecv[y, :, take] = total.astype(BF)
                return 0

            lax.fori_loop(0, HA, add, 0)
            if m:
                a_copy(half, m, yb, y).start()

    def parts_z(k, owner):
        return remote(parts.at[owner], parts.at[owner], pz_s.at[k], pz_r.at[k], along_z(k))

    def parts_y(m, owner):
        return remote(parts_sum.at[block_of(m)], parts_in.at[owner], py_s.at[m], py_r.at[m], along_y(-m))

    wd_own.wait()
    for k in (1, 3, 2):
        wd_copy(k, shifted(z, -k, SLICES)).wait_recv()
    for copy in saved:
        copy.wait()

    def weights_here(c, _):
        for copy in w_copy(c):
            copy.wait()
        return 0

    lax.fori_loop(0, D // CW, weights_here, 0)

    partial_grad(0)
    partial_grad(2)
    relay_grad(0)
    partial_grad(1)
    relay_grad(2)
    partial_grad(3)
    relay_grad(1)
    elementwise(0)
    relay_grad(3)
    input_a(0)
    for m in (2, 1, 3):
        elementwise(m)
        input_b(m)
    for k in (2, 1, 3):
        parts_z(k, z).start()
    input_a(1)
    relay(0)
    input_a(3)
    relay(1)
    input_a(2)
    relay(3)
    input_b(0)
    relay(2)

    for k in (1, 3, 2):
        parts_z(k, shifted(z, -k, SLICES)).wait_recv()
    parts_sum[...] = parts[0] + parts[1] + parts[2] + parts[3]
    for m in (1, 3, 2):
        parts_y(m, y).start()
    parts_in[y] = parts_sum[y]

    def b_first(half, j):
        src = ctok.at[z2, :, cols(j * CW, CW)]
        if half == 0:
            return remote(src, rb1p.at[:, cols(j * CW, CW)], b1_s.at[j], b1_r.at[j], right)
        return remote(src, rb1m.at[:, cols((j - HB) * CW, CW)], b1_s.at[j], b1_r.at[j], left)

    def b_right(j):
        return remote(ctok.at[zp, :, cols(j * CW, CW)], rb2p.at[:, cols(j * CW, CW)], b2p_s.at[j], b2p_r.at[j], right)

    def b_left(j):
        return remote(ctok.at[zm, :, cols(j * CW, CW)], rb2m.at[:, cols(j * CW, CW)], b2m_s.at[j], b2m_r.at[j], left)

    def tokens(half):
        for m in (1, 3, 2):
            b_copy(half, m, block_of(m), shifted(y, m, E_WIN)).wait_recv()

        def chunk(j, _):
            def combine(zz, _):
                rows = brecv[zz, :, :, cols(j * CW, CW)].reshape(E_WIN * CAP, CW)
                ctok[zz, :, cols(j * CW, CW)] = jnp.dot(spread[zz], rows, preferred_element_type=F32).astype(BF)
                return 0

            lax.fori_loop(0, SLICES, combine, 0)
            b_first(half, j).start()
            (b_left, b_right)[half](j).start()
            return 0

        lax.fori_loop(half * HB, (half + 1) * HB, chunk, 0)

    finish(0)
    finish(1)
    finish(3)
    finish(2)
    tokens(0)
    tokens(1)

    def relay_b(half, j):
        b_first(half, j).wait_recv()
        if half == 0:
            mine, other = ctok.at[zp, :, cols(j * CW, CW)], rb1p.at[:, cols(j * CW, CW)]
        else:
            mine, other = ctok.at[zm, :, cols(j * CW, CW)], rb1m.at[:, cols((j - HB) * CW, CW)]
        mine[...] = (mine[...].astype(F32) + other[...].astype(F32)).astype(BF)
        (b_right, b_left)[half](j).start()

    def relay_b_pair(i, _):
        relay_b(0, i)
        relay_b(1, HB + i)
        return 0

    lax.fori_loop(0, HB, relay_b_pair, 0)

    for m in (1, 3, 2):
        parts_y(m, shifted(y, m, E_WIN)).wait_recv()
    for k in range(TOPK):
        router[pl.ds(k, 1)] = jnp.zeros((1, TOK), F32)

    def router_part(e, _):
        row = parts_in[e, pl.ds(z, 1)]
        column = jnp.sum(jnp.where(slot_row == lane_row, row, 0.0), axis=-1, keepdims=True)
        values = jnp.sum(pick[z, e].astype(F32) * column, axis=0, keepdims=True)
        for k in range(TOPK):
            router[pl.ds(k, 1)] += jnp.where(routes[pl.ds(k, 1)] == e, values, 0.0)
        return 0

    lax.fori_loop(0, E_WIN, router_part, 0)

    def out_copy(c):
        return pltpu.make_async_copy(cot.at[:, cols(c * CW, CW)], out.at[:, cols(c * CW, CW)], out_s.at[c])

    cot_copy.wait_recv()
    for half in (0, 1):
        for m in (1, 3, 2):
            a_copy(half, m, block_of(m), shifted(y, m, E_WIN)).wait_recv()

        def last_a(c, _):
            take = cols(c * CW, CW)
            rows = arecv[:, :, take].reshape(E_WIN * CAP, CW)
            total = jnp.dot(spread[z], rows, preferred_element_type=F32)
            cot[:, take] = (cot[:, take].astype(F32) + total).astype(BF)
            out_copy(c).start()
            return 0

        lax.fori_loop(half * HA, (half + 1) * HA, last_a, 0)

    def last_b(j, _):
        b_right(j).wait_recv()
        b_left(j).wait_recv()
        take = cols(j * CW, CW)
        total = ctok[z, :, take].astype(F32) + rb2p[:, take].astype(F32) + rb2m[:, take].astype(F32)
        there = cols(CA + j * CW, CW)
        cot[:, there] = (cot[:, there].astype(F32) + total).astype(BF)
        out_copy(NA + j).start()
        return 0

    lax.fori_loop(0, NB, last_b, 0)

    def written(c, _):
        out_copy(c).wait()
        return 0

    lax.fori_loop(0, D // CW, written, 0)
    cot_copy.wait_send()
    for k in range(1, SLICES):
        info_z(k, z).wait_send()
        info_y(k, y).wait_send()
        wd_copy(k, z).wait_send()
        parts_z(k, z).wait_send()
        parts_y(k, y).wait_send()
    for h in range(NQ - FLY, NQ):
        for k in range(SLICES):
            tok_copy(k, h, z).wait_send()
    for half in (0, 1):
        for m in BLOCKS:
            yb = block_of(m)
            first(half, m, yb).wait_send()
            to_right(half, m, yb).wait_send()
            to_left(half, m, yb).wait_send()
            if m:
                a_copy(half, m, yb, y).wait_send()
                b_copy(half, m, yb, y).wait_send()

    def sent_b(half, j):
        b_first(half, j).wait_send()
        b_right(j).wait_send()
        b_left(j).wait_send()

    def sent_b_pair(i, _):
        sent_b(0, i)
        sent_b(1, HB + i)
        return 0

    lax.fori_loop(0, HB, sent_b_pair, 0)


def vmem(*shape, dtype=BF):
    return pltpu.VMEM(shape, dtype)


def sems(*shape):
    return pltpu.SemaphoreType.DMA(shape)


ANY = pl.BlockSpec(memory_space=pl.ANY)
VM = pl.BlockSpec(memory_space=pltpu.VMEM)


def layer(upstream, routes, gains, gate, up, w_gate, w_up, w_down):
    return pl.pallas_call(
        layer_kernel,
        out_shape=(
            jax.ShapeDtypeStruct((TOK, D), BF),
            jax.ShapeDtypeStruct((TOPK, TOK), F32),
        ),
        in_specs=[ANY, VM, VM, ANY, ANY, ANY, ANY, ANY],
        out_specs=(ANY, VM),
        scratch_shapes=[
            vmem(E_WIN, SLICES, 8, TOK, dtype=F32),
            vmem(E_WIN, SLICES, 8, TOK, dtype=F32),
            vmem(SLICES, E_WIN, CAP, TOK),
            vmem(SLICES, TOK, E_WIN * CAP),
            vmem(E_WIN * SLICES, CAP, HID),
            vmem(E_WIN * SLICES, CAP, HID),
            vmem(SLICES, HID, Q),
            vmem(TOK, D),
            vmem(SLICES, E_WIN, 8, TOK, dtype=F32),
            vmem(E_WIN, 8, TOK, dtype=F32),
            vmem(E_WIN, 8, TOK, dtype=F32),
            vmem(E_WIN, SLICES, CAP, 2 * HID),
            vmem(D // CW, CW, 2 * HID),
            vmem(E_WIN, SLICES, CAP, D),
            vmem(E_WIN, CAP, HALF),
            vmem(E_WIN, CAP, HALF),
            vmem(E_WIN, CAP, CA),
            vmem(E_WIN, CAP, CA),
            vmem(E_WIN, CAP, CA),
            vmem(SLICES, E_WIN, CAP, WB),
            vmem(SLICES, TOK, WB),
            vmem(TOK, HALFB),
            vmem(TOK, HALFB),
            vmem(TOK, WB),
            vmem(TOK, WB),
            sems(SLICES), sems(SLICES),
            sems(E_WIN), sems(E_WIN),
            sems(SLICES, NQ), sems(SLICES, NQ),
            sems(SLICES), sems(SLICES),
            pltpu.SemaphoreType.DMA, pltpu.SemaphoreType.DMA,
            sems(E_WIN, NQ), sems(E_WIN, NQ),
            sems(2, E_WIN), sems(2, E_WIN),
            sems(2, 2, E_WIN), sems(2, 2, E_WIN),
            sems(3),
            sems(D // CW),
            sems(SLICES), sems(SLICES),
            sems(E_WIN), sems(E_WIN),
            sems(2, D // CW),
            sems(2, E_WIN), sems(2, E_WIN),
            sems(2, E_WIN), sems(2, E_WIN),
            sems(2, E_WIN), sems(2, E_WIN),
            sems(2, E_WIN), sems(2, E_WIN),
            sems(2, E_WIN), sems(2, E_WIN),
            sems(NB), sems(NB),
            sems(NB), sems(NB),
            sems(NB), sems(NB),
        ],
        compiler_params=pltpu.CompilerParams(collective_id=0, has_side_effects=True, vmem_limit_bytes=63 * 2**20),
        name="layer",
    )(upstream, routes, gains, gate, up, w_gate, w_up, w_down)


def local(upstream, routes, combine_weights, gate_saved, up_saved, w_gate, w_up, w_down):
    grad_input, router_grad = layer(
        upstream[0], routes[0].T, combine_weights[0].T, gate_saved[0], up_saved[0], w_gate[0], w_up[0], w_down[0]
    )
    return grad_input[None], router_grad.T[None]


def solution(mesh):
    in_specs = (
        P("section", "ep", None),
        P("section", "ep", None),
        P("section", "ep", None),
        P("section", None, None, "ep"),
        P("section", None, None, "ep"),
        P("section", None, "ep"),
        P("section", None, "ep"),
        P("section", "ep", None),
    )
    out_specs = (P("section", "ep", None), P("section", "ep", None))
    return jax.shard_map(local, mesh=mesh, in_specs=in_specs, out_specs=out_specs, check_vma=False)
```

time: 234 us -> 217 us (0.927)
  Pallas kernels: 229 us -> 213 us
    pallas_call x1, Pallas kernels: 229 us -> 213 us  [layer(): pl.pallas_call(layer_kernel, out_shape=(jax.ShapeDtypeStruct((TOK, D), BF...]
where the time goes in v3:
time: 217 us
  Pallas kernels  213 us (98%)
  local copies, waits for them, and re-layouts  3.41 us (2%)
    pallas_call x1, Pallas kernels, layer(): pl.pallas_call(layer_kernel, out_shape=(jax.ShapeDtypeStruct((TOK, D), BF...  213 us

profile of v3, /device:TPU:7, one launch (start us, length us, event | category | flops | bytes accessed | tf_op | source)
XLA Modules:
  0.0 217.2 jit_solution(12255377320739021593)
XLA Ops:
  0.6 213.1 %layer.1 = (bf16[128,7168]{1,0:T(8,128)(2,1)}, f32[2,128]{1,0:T(2,128)}) custom-call(bf16[128,7168]{1,0:T(8,128)(2,1)} %bitcast.20, s32[2,128]{1,0:T(2,128)} %bitcast.23, bf16[2,128]{1,0:T(2,128)(2,1)} %bitcast.25, bf16[16,80,256]{2,1,0:T(8,128)(2,1)} %bitcast.21, bf16[16,80,256]{2,1,0:T(8,128)(2,1)} %bitcast.22, bf16[7168,256]{1,0:T(8,128)(2,1)} %bitcast.16, ...), custom_call_target="tpu_custom_call" | custom-call | tf_op jit(solution)/shard_map/layer/pallas_call | solution.py:609
  213.7 0.0 copy-start
  213.7 2.8 %copy.12 = bf16[1,128,7168]{2,1,0:T(8,128)(2,1)} copy(bf16[1,128,7168]{2,1,0:T(8,128)(2,1)} %bitcast.19) | data formatting | bytes 3670016
  216.6 0.0 copy-done
  216.6 0.6 copy.13
Async XLA Ops:
  213.7 2.9 %copy-start = (f32[2,128]{1,0:T(2,128)S(1)}, f32[2,128]{1,0:T(2,128)}, u32[]{:S(2)}) copy-start(f32[2,128]{1,0:T(2,128)} %get-tuple-element.5) | copy-start | bytes 3076

commit v4 on v3

--- a/solution.py
+++ b/solution.py
@@ -21,18 +21,20 @@
 ROWS = SLICES * CAP
 NQ = 7
 QH = Q // NQ
-FLY = 3
-
+FLY = 6
+
+CA = 1024
+WB = D - CA
 CW = 512
-CA = 4096
-NA = CA // CW
-HA = NA // 2
-HALF = CA // 2
-WB = D - CA
-NB = WB // CW
-HB = NB // 2
-HALFB = WB // 2
+FAR_W = D // 4
+NEAR_W = CA // 2
+BW = WB // 4
+BC = BW // 2
 BLOCKS = (0, 1, 3, 2)
+NEAR = (0, 1, 3)
+FAR_PIECES = [(2, n // 2, n * FAR_W, FAR_W, n) for n in range(4)]
+NEAR_PIECES = [(m, n, n * NEAR_W, NEAR_W, 4 + 2 * NEAR.index(m) + n) for m in (1, 3, 0) for n in range(2)]
+PIECES = FAR_PIECES + NEAR_PIECES
 
 
 def dot_nt(a, b):
@@ -61,8 +63,8 @@
 
 def layer_kernel(
     up, routes, gains, gate, upv, wg, wu, wd, out, router,
-    info, slot_gain, pick, spread, gate_v, up_v, wdr, cot, parts, parts_sum, parts_in,
-    grads, weights, partial, r1p, r1m, r2p, r2m, arecv, brecv, ctok, rb1p, rb1m, rb2p, rb2m,
+    info, slot_gain, pick, spread_near, spread_far, gate_v, up_v, wdr, cot, parts, parts_sum, parts_in,
+    grads, weights, partial, r1f, r1n, r2pf, r2pn, r2mf, r2mn, af, an, brecv, ctok, rb1, rb2p, rb2m,
     iz_s, iz_r, iy_s, iy_r, tok_s, tok_r, wd_s, wd_r, cot_s, cot_r, y_s, y_r,
     g1_s, g1_r, g2_s, g2_r, loc, out_s, pz_s, pz_r, py_s, py_r,
     w_sem, r1_s, r1_r, r2p_s, r2p_r, r2m_s, r2m_r, ay_s, ay_r, by_s, by_r, b1_s, b1_r, b2p_s, b2p_r, b2m_s, b2m_r,
@@ -90,8 +92,8 @@
     def w_copy(c):
         take = pl.ds(c * CW, CW)
         return (
-            pltpu.make_async_copy(wg.at[take], weights.at[c, :, pl.ds(0, HID)], w_sem.at[0, c]),
-            pltpu.make_async_copy(wu.at[take], weights.at[c, :, pl.ds(HID, HID)], w_sem.at[1, c]),
+            pltpu.make_async_copy(wg.at[take], weights.at[take, pl.ds(0, HID)], w_sem.at[0, c]),
+            pltpu.make_async_copy(wu.at[take], weights.at[take, pl.ds(HID, HID)], w_sem.at[1, c]),
         )
 
     wd_own = pltpu.make_async_copy(wd.at[:, cols(z * Q, Q)], wdr.at[z], loc.at[0])
@@ -172,6 +174,7 @@
     for h in range(FLY):
         for k in (2, 1, 3, 0):
             tok_copy(k, h, z).start()
+    wd_copy(2, z).start()
     wd_own.start()
     for copy in saved:
         copy.start()
@@ -226,7 +229,7 @@
         return 0
 
     lax.fori_loop(0, NQ - FLY, dispatch, 0)
-    for k in (2, 1, 3):
+    for k in (1, 3):
         wd_copy(k, z).start()
     cot_copy.start()
 
@@ -252,10 +255,12 @@
     lax.fori_loop(0, E_WIN * SLICES, expert_tables, 0)
 
     def spread_tables(zz, _):
-        spread[zz] = dot_nt(unit, pick[zz].reshape(E_WIN * CAP, TOK)).astype(BF)
+        rows = jnp.concatenate([pick[zz, shifted(y, m, E_WIN)] for m in NEAR], axis=0)
+        spread_near[zz] = dot_nt(unit, rows).astype(BF)
         return 0
 
     lax.fori_loop(0, SLICES, spread_tables, 0)
+    spread_far[...] = dot_nt(unit, pick[z, shifted(y, 2, E_WIN)]).astype(BF)
 
     def block_of(m):
         return shifted(y, -m, E_WIN)
@@ -317,96 +322,104 @@
             for h in range(NQ):
                 y_copy((E_WIN - m) % E_WIN, h, y).wait_send()
 
-    def first(half, m, yb):
-        src = partial.at[yb, z2, :, pl.ds(half * HALF, HALF)]
-        return remote(src, (r1p, r1m)[half].at[yb], r1_s.at[half, m], r1_r.at[half, m], (right, left)[half])
-
-    def to_right(half, m, yb):
-        take = pl.ds(half * HALF, HALF)
-        return remote(partial.at[yb, zp, :, take], r2p.at[yb, :, take], r2p_s.at[half, m], r2p_r.at[half, m], right)
-
-    def to_left(half, m, yb):
-        take = pl.ds(half * HALF, HALF)
-        return remote(partial.at[yb, zm, :, take], r2m.at[yb, :, take], r2m_s.at[half, m], r2m_r.at[half, m], left)
-
-    def a_copy(half, m, yb, owner):
-        take = pl.ds(half * HALF, HALF)
+    def there(far, near, piece):
+        m, _, col, width, _ = piece
+        if m == 2:
+            return far.at[:, pl.ds(col, width)]
+        return near.at[NEAR.index(m), :, pl.ds(col, width)]
+
+    def mine(piece, zz):
+        m, _, col, width, _ = piece
+        return partial.at[block_of(m), zz, :, pl.ds(col, width)]
+
+    def first(piece):
+        half, i = piece[1], piece[4]
+        return remote(mine(piece, z2), there(r1f, r1n, piece), r1_s.at[i], r1_r.at[i], (right, left)[half])
+
+    def second(side, piece):
+        i = piece[4]
+        if side == 0:
+            return remote(mine(piece, zp), there(r2pf, r2pn, piece), r2p_s.at[i], r2p_r.at[i], right)
+        return remote(mine(piece, zm), there(r2mf, r2mn, piece), r2m_s.at[i], r2m_r.at[i], left)
+
+    def a_copy(piece):
+        m, i = piece[0], piece[4]
+        return remote(mine(piece, z), there(af, an, piece), ay_s.at[i], ay_r.at[i], along_y(-m))
+
+    def product(m, col, width, steps):
+        yb = block_of(m)
+
+        def chunk(c, _):
+            take = cols(col + c * width, width)
+            part = dot_nt(grads[yb].reshape(ROWS, 2 * HID), weights[pl.ds(pl.multiple_of(col + c * width, 128), width)])
+            partial[yb, :, :, take] = part.astype(BF).reshape(SLICES, CAP, width)
+            return 0
+
+        lax.fori_loop(0, steps, chunk, 0)
+
+    def produce(piece):
+        m, half, col, width, _ = piece
+        if m == 2:
+            product(m, col, width // 2, 2)
+        else:
+            product(m, col, width, 1)
+        first(piece).start()
+        second(1 - half, piece).start()
+
+    def relay(piece):
+        half, width = piece[1], piece[3]
+        first(piece).wait_recv()
+        here, other = mine(piece, (zp, zm)[half]), there(r1f, r1n, piece)
+        step = width // 2
+
+        def add(c, _):
+            take = cols(c * step, step)
+            here[:, take] = (here[:, take].astype(F32) + other[:, take].astype(F32)).astype(BF)
+            return 0
+
+        lax.fori_loop(0, 2, add, 0)
+        second(half, piece).start()
+
+    def finish(piece):
+        m, width = piece[0], piece[3]
+        second(0, piece).wait_recv()
+        second(1, piece).wait_recv()
+        here, one, two = mine(piece, z), there(r2pf, r2pn, piece), there(r2mf, r2mn, piece)
+        dest = here if m else there(af, an, piece)
+        step = width // 2
+
+        def add(c, _):
+            take = cols(c * step, step)
+            total = here[:, take].astype(F32) + one[:, take].astype(F32) + two[:, take].astype(F32)
+            dest[:, take] = total.astype(BF)
+            return 0
+
+        lax.fori_loop(0, 2, add, 0)
+
+    def b_copy(p, m):
         return remote(
-            partial.at[yb, z, :, take], arecv.at[owner, :, take], ay_s.at[half, m], ay_r.at[half, m], along_y(-m)
+            partial.at[block_of(m), :, :, pl.ds(CA + p * BW, BW)],
+            brecv.at[:, NEAR.index(m), :, pl.ds(p * BW, BW)],
+            by_s.at[p, m], by_r.at[p, m], along_y(-m),
         )
 
-    def b_copy(half, m, yb, owner):
-        return remote(
-            partial.at[yb, :, :, pl.ds(CA + half * HALFB, HALFB)],
-            brecv.at[:, owner, :, pl.ds(half * HALFB, HALFB)],
-            by_s.at[half, m], by_r.at[half, m], along_y(-m),
-        )
-
-    def chunks_of(m, start, stop):
-        yb = block_of(m)
-
-        def chunk(c, _):
-            part = dot_nt(grads[yb].reshape(ROWS, 2 * HID), weights[c])
-            partial[yb, :, :, cols(c * CW, CW)] = part.astype(BF).reshape(SLICES, CAP, CW)
-            return 0
-
-        lax.fori_loop(start, stop, chunk, 0)
-        return yb
-
-    def input_a(m):
-        yb = chunks_of(m, 0, HA)
-        first(0, m, yb).start()
-        to_left(0, m, yb).start()
-        chunks_of(m, HA, NA)
-        first(1, m, yb).start()
-        to_right(1, m, yb).start()
-
-    def input_b(m):
-        for half in (0, 1):
-            yb = chunks_of(m, NA + half * HB, NA + (half + 1) * HB)
-            if m:
-                b_copy(half, m, yb, y).start()
+    def b_start(p):
+        for m in (1, 3):
+            b_copy(p, m).start()
+
+    def b_sent(p):
+        for m in (1, 3):
+            b_copy(p, m).wait_send()
+
+    def produce_b(p, m):
+        product(m, CA + p * BW, BC, 2)
         if m == 0:
 
             def keep(zz, _):
-                brecv[zz, y] = partial[y, zz, :, pl.ds(CA, WB)]
+                brecv[zz, 0, :, pl.ds(p * BW, BW)] = partial[y, zz, :, pl.ds(CA + p * BW, BW)]
                 return 0
 
             lax.fori_loop(0, SLICES, keep, 0)
-
-    def relay(m):
-        yb = block_of(m)
-        for half in (0, 1):
-            first(half, m, yb).wait_recv()
-
-            def add(c, _):
-                mine = partial.at[yb, (zp, zm)[half], :, cols(half * HALF + c * CW, CW)]
-                other = (r1p, r1m)[half][yb, :, cols(c * CW, CW)]
-                mine[...] = (mine[...].astype(F32) + other.astype(F32)).astype(BF)
-                return 0
-
-            lax.fori_loop(0, HA, add, 0)
-            (to_right, to_left)[half](half, m, yb).start()
-
-    def finish(m):
-        yb = block_of(m)
-        for half in (0, 1):
-            to_right(half, m, yb).wait_recv()
-            to_left(half, m, yb).wait_recv()
-
-            def add(c, _):
-                take = cols(half * HALF + c * CW, CW)
-                mine = partial.at[yb, z, :, take]
-                total = mine[...].astype(F32) + r2p[yb, :, take].astype(F32) + r2m[yb, :, take].astype(F32)
-                if m:
-                    mine[...] = total.astype(BF)
-                else:
-                    arecv[y, :, take] = total.astype(BF)
-                return 0
-
-            lax.fori_loop(0, HA, add, 0)
-            if m:
-                a_copy(half, m, yb, y).start()
 
     def parts_z(k, owner):
         return remote(parts.at[owner], parts.at[owner], pz_s.at[k], pz_r.at[k], along_z(k))
@@ -427,29 +440,79 @@
 
     lax.fori_loop(0, D // CW, weights_here, 0)
 
-    partial_grad(0)
-    partial_grad(2)
-    relay_grad(0)
+    def b_first(p):
+        take = pl.ds(p * BW, BW)
+        return remote(ctok.at[z2, :, take], rb1.at[:, take], b1_s.at[p], b1_r.at[p], (right, left)[p // 2])
+
+    def b_second(side, p):
+        take = pl.ds(p * BW, BW)
+        if side == 0:
+            return remote(ctok.at[zp, :, take], rb2p.at[:, take], b2p_s.at[p], b2p_r.at[p], right)
+        return remote(ctok.at[zm, :, take], rb2m.at[:, take], b2m_s.at[p], b2m_r.at[p], left)
+
+    def tokens(p):
+        for m in (1, 3):
+            b_copy(p, m).wait_recv()
+
+        def combine(i, _):
+            zz, take = i // 2, cols(p * BW + lax.rem(i, 2) * BC, BC)
+            rows = brecv[zz, :, :, take].reshape(len(NEAR) * CAP, BC)
+            ctok[zz, :, take] = jnp.dot(spread_near[zz], rows, preferred_element_type=F32).astype(BF)
+            return 0
+
+        lax.fori_loop(0, 2 * SLICES, combine, 0)
+        b_first(p).start()
+        b_second(1 - p // 2, p).start()
+
+    def relay_b(p):
+        b_first(p).wait_recv()
+
+        def add(c, _):
+            take = cols(p * BW + c * BC, BC)
+            here = ctok.at[(zp, zm)[p // 2], :, take]
+            here[...] = (here[...].astype(F32) + rb1[:, take].astype(F32)).astype(BF)
+            return 0
+
+        lax.fori_loop(0, 2, add, 0)
+        b_second(p // 2, p).start()
+
     partial_grad(1)
-    relay_grad(2)
     partial_grad(3)
     relay_grad(1)
+    partial_grad(2)
+    relay_grad(3)
+    elementwise(1)
+    relay_grad(2)
+    partial_grad(0)
+    elementwise(3)
+    produce_b(0, 1)
+    produce_b(0, 3)
+    b_start(0)
+    relay_grad(0)
+    elementwise(2)
+    produce(FAR_PIECES[0])
+    produce(FAR_PIECES[2])
+    produce_b(2, 1)
+    produce_b(2, 3)
+    b_start(2)
+    produce(FAR_PIECES[1])
+    produce(FAR_PIECES[3])
     elementwise(0)
-    relay_grad(3)
-    input_a(0)
-    for m in (2, 1, 3):
-        elementwise(m)
-        input_b(m)
     for k in (2, 1, 3):
         parts_z(k, z).start()
-    input_a(1)
-    relay(0)
-    input_a(3)
-    relay(1)
-    input_a(2)
-    relay(3)
-    input_b(0)
-    relay(2)
+    for piece in NEAR_PIECES:
+        produce(piece)
+    for p in (1, 3):
+        for m in (1, 3):
+            produce_b(p, m)
+    relay(FAR_PIECES[0])
+    relay(FAR_PIECES[2])
+    for p in range(4):
+        produce_b(p, 0)
+    relay(FAR_PIECES[1])
+    relay(FAR_PIECES[3])
+    for piece in NEAR_PIECES:
+        relay(piece)
 
     for k in (1, 3, 2):
         parts_z(k, shifted(z, -k, SLICES)).wait_recv()
@@ -458,57 +521,28 @@
         parts_y(m, y).start()
     parts_in[y] = parts_sum[y]
 
-    def b_first(half, j):
-        src = ctok.at[z2, :, cols(j * CW, CW)]
-        if half == 0:
-            return remote(src, rb1p.at[:, cols(j * CW, CW)], b1_s.at[j], b1_r.at[j], right)
-        return remote(src, rb1m.at[:, cols((j - HB) * CW, CW)], b1_s.at[j], b1_r.at[j], left)
-
-    def b_right(j):
-        return remote(ctok.at[zp, :, cols(j * CW, CW)], rb2p.at[:, cols(j * CW, CW)], b2p_s.at[j], b2p_r.at[j], right)
-
-    def b_left(j):
-        return remote(ctok.at[zm, :, cols(j * CW, CW)], rb2m.at[:, cols(j * CW, CW)], b2m_s.at[j], b2m_r.at[j], left)
-
-    def tokens(half):
-        for m in (1, 3, 2):
-            b_copy(half, m, block_of(m), shifted(y, m, E_WIN)).wait_recv()
-
-        def chunk(j, _):
-            def combine(zz, _):
-                rows = brecv[zz, :, :, cols(j * CW, CW)].reshape(E_WIN * CAP, CW)
-                ctok[zz, :, cols(j * CW, CW)] = jnp.dot(spread[zz], rows, preferred_element_type=F32).astype(BF)
-                return 0
-
-            lax.fori_loop(0, SLICES, combine, 0)
-            b_first(half, j).start()
-            (b_left, b_right)[half](j).start()
-            return 0
-
-        lax.fori_loop(half * HB, (half + 1) * HB, chunk, 0)
-
-    finish(0)
-    finish(1)
-    finish(3)
-    finish(2)
+    b_sent(0)
+    b_start(1)
+    b_sent(2)
+    b_start(3)
     tokens(0)
+    tokens(2)
+    for n in (0, 2, 1, 3):
+        finish(FAR_PIECES[n])
+    relay_b(0)
+    relay_b(2)
+    b_sent(1)
+    b_sent(3)
+    for n in (0, 2, 1, 3):
+        a_copy(FAR_PIECES[n]).start()
     tokens(1)
-
-    def relay_b(half, j):
-        b_first(half, j).wait_recv()
-        if half == 0:
-            mine, other = ctok.at[zp, :, cols(j * CW, CW)], rb1p.at[:, cols(j * CW, CW)]
-        else:
-            mine, other = ctok.at[zm, :, cols(j * CW, CW)], rb1m.at[:, cols((j - HB) * CW, CW)]
-        mine[...] = (mine[...].astype(F32) + other[...].astype(F32)).astype(BF)
-        (b_right, b_left)[half](j).start()
-
-    def relay_b_pair(i, _):
-        relay_b(0, i)
-        relay_b(1, HB + i)
-        return 0
-
-    lax.fori_loop(0, HB, relay_b_pair, 0)
+    tokens(3)
+    for piece in NEAR_PIECES:
+        finish(piece)
+        if piece[0]:
+            a_copy(piece).start()
+    relay_b(1)
+    relay_b(3)
 
     for m in (1, 3, 2):
         parts_y(m, shifted(y, m, E_WIN)).wait_recv()
@@ -529,31 +563,36 @@
         return pltpu.make_async_copy(cot.at[:, cols(c * CW, CW)], out.at[:, cols(c * CW, CW)], out_s.at[c])
 
     cot_copy.wait_recv()
-    for half in (0, 1):
-        for m in (1, 3, 2):
-            a_copy(half, m, block_of(m), shifted(y, m, E_WIN)).wait_recv()
-
-        def last_a(c, _):
-            take = cols(c * CW, CW)
-            rows = arecv[:, :, take].reshape(E_WIN * CAP, CW)
-            total = jnp.dot(spread[z], rows, preferred_element_type=F32)
-            cot[:, take] = (cot[:, take].astype(F32) + total).astype(BF)
-            out_copy(c).start()
+    for piece in PIECES:
+        if piece[0]:
+            a_copy(piece).wait_recv()
+
+    def far_rows(take):
+        return cot[:, take].astype(F32) + jnp.dot(spread_far[...], af[:, take], preferred_element_type=F32)
+
+    def last_a(c, _):
+        take = cols(c * CW, CW)
+        rows = an[:, :, take].reshape(len(NEAR) * CAP, CW)
+        total = jnp.dot(spread_near[z], rows, preferred_element_type=F32)
+        cot[:, take] = (far_rows(take) + total).astype(BF)
+        out_copy(c).start()
+        return 0
+
+    lax.fori_loop(0, CA // CW, last_a, 0)
+
+    for p in (0, 2, 1, 3):
+        b_second(0, p).wait_recv()
+        b_second(1, p).wait_recv()
+
+        def last_b(c, _):
+            here = cols(p * BW + c * CW, CW)
+            take = cols(CA + p * BW + c * CW, CW)
+            total = ctok[z, :, here].astype(F32) + rb2p[:, here].astype(F32) + rb2m[:, here].astype(F32)
+            cot[:, take] = (far_rows(take) + total).astype(BF)
+            out_copy((CA + p * BW) // CW + c).start()
             return 0
 
-        lax.fori_loop(half * HA, (half + 1) * HA, last_a, 0)
-
-    def last_b(j, _):
-        b_right(j).wait_recv()
-        b_left(j).wait_recv()
-        take = cols(j * CW, CW)
-        total = ctok[z, :, take].astype(F32) + rb2p[:, take].astype(F32) + rb2m[:, take].astype(F32)
-        there = cols(CA + j * CW, CW)
-        cot[:, there] = (cot[:, there].astype(F32) + total).astype(BF)
-        out_copy(NA + j).start()
-        return 0
-
-    lax.fori_loop(0, NB, last_b, 0)
+        lax.fori_loop(0, BW // CW, last_b, 0)
 
     def written(c, _):
         out_copy(c).wait()
@@ -570,27 +609,16 @@
     for h in range(NQ - FLY, NQ):
         for k in range(SLICES):
             tok_copy(k, h, z).wait_send()
-    for half in (0, 1):
-        for m in BLOCKS:
-            yb = block_of(m)
-            first(half, m, yb).wait_send()
-            to_right(half, m, yb).wait_send()
-            to_left(half, m, yb).wait_send()
-            if m:
-                a_copy(half, m, yb, y).wait_send()
-                b_copy(half, m, yb, y).wait_send()
-
-    def sent_b(half, j):
-        b_first(half, j).wait_send()
-        b_right(j).wait_send()
-        b_left(j).wait_send()
-
-    def sent_b_pair(i, _):
-        sent_b(0, i)
-        sent_b(1, HB + i)
-        return 0
-
-    lax.fori_loop(0, HB, sent_b_pair, 0)
+    for piece in PIECES:
+        first(piece).wait_send()
+        second(0, piece).wait_send()
+        second(1, piece).wait_send()
+        if piece[0]:
+            a_copy(piece).wait_send()
+    for p in range(4):
+        b_first(p).wait_send()
+        b_second(0, p).wait_send()
+        b_second(1, p).wait_send()
 
 
 def vmem(*shape, dtype=BF):
@@ -618,7 +646,8 @@
             vmem(E_WIN, SLICES, 8, TOK, dtype=F32),
             vmem(E_WIN, SLICES, 8, TOK, dtype=F32),
             vmem(SLICES, E_WIN, CAP, TOK),
-            vmem(SLICES, TOK, E_WIN * CAP),
+            vmem(SLICES, TOK, len(NEAR) * CAP),
+            vmem(TOK, CAP),
             vmem(E_WIN * SLICES, CAP, HID),
             vmem(E_WIN * SLICES, CAP, HID),
             vmem(SLICES, HID, Q),
@@ -627,17 +656,15 @@
             vmem(E_WIN, 8, TOK, dtype=F32),
             vmem(E_WIN, 8, TOK, dtype=F32),
             vmem(E_WIN, SLICES, CAP, 2 * HID),
-            vmem(D // CW, CW, 2 * HID),
+            vmem(D, 2 * HID),
             vmem(E_WIN, SLICES, CAP, D),
-            vmem(E_WIN, CAP, HALF),
-            vmem(E_WIN, CAP, HALF),
-            vmem(E_WIN, CAP, CA),
-            vmem(E_WIN, CAP, CA),
-            vmem(E_WIN, CAP, CA),
-            vmem(SLICES, E_WIN, CAP, WB),
+            vmem(CAP, D), vmem(len(NEAR), CAP, CA),
+            vmem(CAP, D), vmem(len(NEAR), CAP, CA),
+            vmem(CAP, D), vmem(len(NEAR), CAP, CA),
+            vmem(CAP, D), vmem(len(NEAR), CAP, CA),
+            vmem(SLICES, len(NEAR), CAP, WB),
             vmem(SLICES, TOK, WB),
-            vmem(TOK, HALFB),
-            vmem(TOK, HALFB),
+            vmem(TOK, WB),
             vmem(TOK, WB),
             vmem(TOK, WB),
             sems(SLICES), sems(SLICES),
@@ -653,14 +680,14 @@
             sems(SLICES), sems(SLICES),
             sems(E_WIN), sems(E_WIN),
             sems(2, D // CW),
-            sems(2, E_WIN), sems(2, E_WIN),
-            sems(2, E_WIN), sems(2, E_WIN),
-            sems(2, E_WIN), sems(2, E_WIN),
-            sems(2, E_WIN), sems(2, E_WIN),
-            sems(2, E_WIN), sems(2, E_WIN),
-            sems(NB), sems(NB),
-            sems(NB), sems(NB),
-            sems(NB), sems(NB),
+            sems(len(PIECES)), sems(len(PIECES)),
+            sems(len(PIECES)), sems(len(PIECES)),
+            sems(len(PIECES)), sems(len(PIECES)),
+            sems(len(PIECES)), sems(len(PIECES)),
+            sems(4, E_WIN), sems(4, E_WIN),
+            sems(4), sems(4),
+            sems(4), sems(4),
+            sems(4), sems(4),
         ],
         compiler_params=pltpu.CompilerParams(collective_id=0, has_side_effects=True, vmem_limit_bytes=63 * 2**20),
         name="layer",

time: 217 us -> 213 us (0.982)
  Pallas kernels: 213 us -> 208 us
    pallas_call x1, Pallas kernels: 213 us -> 208 us  [layer(): pl.pallas_call(layer_kernel, out_shape=(jax.ShapeDtypeStruct((TOK, D), BF...]
where the time goes in v4:
time: 213 us; the launch traced here: 212 us
  Pallas kernels  208 us (98%)
  local copies, waits for them, and re-layouts  3.41 us (2%)
    pallas_call x1, Pallas kernels, layer(): pl.pallas_call(layer_kernel, out_shape=(jax.ShapeDtypeStruct((TOK, D), BF...  208 us

profile of v4, /device:TPU:7, one launch (start us, length us, event | category | flops | bytes accessed | tf_op | source)
XLA Modules:
  0.0 211.6 jit_solution(3830961040748325087)
XLA Ops:
  0.6 207.6 %layer.1 = (bf16[128,7168]{1,0:T(8,128)(2,1)}, f32[2,128]{1,0:T(2,128)}) custom-call(bf16[128,7168]{1,0:T(8,128)(2,1)} %bitcast.20, s32[2,128]{1,0:T(2,128)} %bitcast.23, bf16[2,128]{1,0:T(2,128)(2,1)} %bitcast.25, bf16[16,80,256]{2,1,0:T(8,128)(2,1)} %bitcast.21, bf16[16,80,256]{2,1,0:T(8,128)(2,1)} %bitcast.22, bf16[7168,256]{1,0:T(8,128)(2,1)} %bitcast.16, ...), custom_call_target="tpu_custom_call" | custom-call | tf_op jit(solution)/shard_map/layer/pallas_call | solution.py:637
  208.2 0.0 copy-start
  208.2 2.8 %copy.12 = bf16[1,128,7168]{2,1,0:T(8,128)(2,1)} copy(bf16[1,128,7168]{2,1,0:T(8,128)(2,1)} %bitcast.19) | data formatting | bytes 3670016
  211.1 0.0 copy-done
  211.1 0.6 copy.13
Async XLA Ops:
  208.2 2.9 %copy-start = (f32[2,128]{1,0:T(2,128)S(1)}, f32[2,128]{1,0:T(2,128)}, u32[]{:S(2)}) copy-start(f32[2,128]{1,0:T(2,128)} %get-tuple-element.5) | copy-start | bytes 3076

commit v5 on v4

--- a/solution.py
+++ b/solution.py
@@ -563,10 +563,6 @@
         return pltpu.make_async_copy(cot.at[:, cols(c * CW, CW)], out.at[:, cols(c * CW, CW)], out_s.at[c])
 
     cot_copy.wait_recv()
-    for piece in PIECES:
-        if piece[0]:
-            a_copy(piece).wait_recv()
-
     def far_rows(take):
         return cot[:, take].astype(F32) + jnp.dot(spread_far[...], af[:, take], preferred_element_type=F32)
 
@@ -578,9 +574,14 @@
         out_copy(c).start()
         return 0
 
-    lax.fori_loop(0, CA // CW, last_a, 0)
-
     for p in (0, 2, 1, 3):
+        for n in {0: (0, 1), 2: (2, 3)}.get(p, ()):
+            a_copy(FAR_PIECES[n]).wait_recv()
+        if p == 1:
+            for piece in NEAR_PIECES:
+                if piece[0]:
+                    a_copy(piece).wait_recv()
+            lax.fori_loop(0, CA // CW, last_a, 0)
         b_second(0, p).wait_recv()
         b_second(1, p).wait_recv()
 

time: 213 us -> 212 us (level)
  no operation moved by 1% of the time
where the time goes in v5:
time: 212 us; the launch traced here: 211 us
  Pallas kernels  206 us (97%)
  local copies, waits for them, and re-layouts  3.41 us (2%)
    pallas_call x1, Pallas kernels, layer(): pl.pallas_call(layer_kernel, out_shape=(jax.ShapeDtypeStruct((TOK, D), BF...  206 us

profile of v5, /device:TPU:7, one launch (start us, length us, event | category | flops | bytes accessed | tf_op | source)
XLA Modules:
  0.0 210.6 jit_solution(18227320617996016715)
XLA Ops:
  0.6 206.5 %layer.1 = (bf16[128,7168]{1,0:T(8,128)(2,1)}, f32[2,128]{1,0:T(2,128)}) custom-call(bf16[128,7168]{1,0:T(8,128)(2,1)} %bitcast.20, s32[2,128]{1,0:T(2,128)} %bitcast.23, bf16[2,128]{1,0:T(2,128)(2,1)} %bitcast.25, bf16[16,80,256]{2,1,0:T(8,128)(2,1)} %bitcast.21, bf16[16,80,256]{2,1,0:T(8,128)(2,1)} %bitcast.22, bf16[7168,256]{1,0:T(8,128)(2,1)} %bitcast.16, ...), custom_call_target="tpu_custom_call" | custom-call | tf_op jit(solution)/shard_map/layer/pallas_call | solution.py:638
  207.1 0.0 copy-start
  207.1 2.8 %copy.12 = bf16[1,128,7168]{2,1,0:T(8,128)(2,1)} copy(bf16[1,128,7168]{2,1,0:T(8,128)(2,1)} %bitcast.19) | data formatting | bytes 3670016
  210.0 0.0 copy-done
  210.0 0.6 copy.13
Async XLA Ops:
  207.1 2.9 %copy-start = (f32[2,128]{1,0:T(2,128)S(1)}, f32[2,128]{1,0:T(2,128)}, u32[]{:S(2)}) copy-start(f32[2,128]{1,0:T(2,128)} %get-tuple-element.5) | copy-start | bytes 3076
